TPU v7x, 256 devices: a whole 4x4x8 slice. The times are simulated.
256 devices in a mesh: tile: 32 (over z, y), zbin: 8 (over x, core).
Axes of the slice: x: 4, y: 4, z: 8, core: 2. Of those that a mesh axis runs over, the one named last changes fastest.
Arguments:
- shear: float32 [8, 2, 1024], P('zbin', None, 'tile'), may hold values from -1.5 to 1.5
- weight: float32 [8, 1024], P('zbin', 'tile'), may hold values from 0.25 to 4
- partner_tiles: int32 [32, 4], P('tile'), may hold values from 0 to 31, as said below
- pair_count: int32 [32], P('tile'), may hold values from 1 to 4, as said below
- pair_bin: int32 [8, 8192, 128], P('zbin', 'tile'), may hold values from 0 to 24
- pair_angle: float32 [8, 8192, 128], P('zbin', 'tile'), may hold values from -3.140625 to 3.140625
Outputs:
- triples: float32 [8, 32, 73728], P('zbin', 'tile')
Inputs may be any that keep to these rules, and one draw needn't show every extreme that they name: `partner_tiles`: slot 0 of each row is the tile itself; the other slots name distinct other tiles. `pair_count`: some tile uses all 4 slots and some tile only its own.
All inputs are finite; a program needn't handle non-finite values.
Results may differ from a plain program's by a relative error of at most 0.0064.
Values may be sent and summed in bfloat16 or wider, within the bound.
A program may use at most 256 MiB of HBM per device.

v0:
```python
import jax
import jax.numpy as jnp
from jax import lax
from jax.sharding import PartitionSpec as P

GAL = 32
NM = 32
NR = 24


def slot_terms(angles, bins, source, live):
    orders = jnp.arange(NM).astype(jnp.float32)
    phase = angles[:, :, None] * orders[None, None, :]
    cosine = jnp.cos(phase)
    sine = jnp.sin(phase)
    first = source[0][None, :, None]
    second = source[1][None, :, None]
    scaled = (source[2] * live)[None, :, None]
    real_part = scaled * (first * cosine + second * sine)
    imag_part = scaled * (second * cosine - first * sine)
    terms = jnp.stack([real_part, imag_part], axis=2).astype(jnp.bfloat16)
    levels = jnp.arange(NR)
    onehot = (bins[:, :, None] == levels[None, None, :]).astype(jnp.bfloat16)
    return jnp.einsum("ijb,ijpn->ibpn", onehot, terms, preferred_element_type=jnp.float32)


def rotate(grid, catalogue):
    real_in = grid[:, :, :, 0, :]
    imag_in = grid[:, :, :, 1, :]
    first = catalogue[0][None, :, None, None]
    second = catalogue[1][None, :, None, None]
    scaled = catalogue[2][None, :, None, None]
    real_wide = real_in.astype(jnp.float32)
    imag_wide = imag_in.astype(jnp.float32)
    upper_real = (scaled * (first * real_wide - second * imag_wide)).astype(jnp.bfloat16)
    upper_imag = (scaled * (first * imag_wide + second * real_wide)).astype(jnp.bfloat16)
    return (real_in, imag_in, upper_real, upper_imag)


def products(parts, number):
    real_in, imag_in, upper_real, upper_imag = parts
    real_out = jnp.einsum(
        "zibn,yicn->nzbyc", upper_real, real_in, preferred_element_type=jnp.float32
    ) + jnp.einsum("zibn,yicn->nzbyc", upper_imag, imag_in, preferred_element_type=jnp.float32)
    imag_out = jnp.einsum(
        "zibn,yicn->nzbyc", upper_imag, real_in, preferred_element_type=jnp.float32
    ) - jnp.einsum("zibn,yicn->nzbyc", upper_real, imag_in, preferred_element_type=jnp.float32)
    legs = upper_real.shape[0] * upper_real.shape[2]
    return jnp.stack([real_out, imag_out], axis=1).reshape(number, 2 * legs * legs)


def per_device(shear, weight, partner_tiles, pair_count, pair_bin, pair_angle):
    gal_rows = shear.shape[2]
    slots = partner_tiles.shape[1]
    centres = pair_bin.shape[1]
    zbins = lax.axis_size("zbin")
    tiles = lax.axis_size("tile")
    packed = jnp.concatenate([shear[0], weight], axis=0)
    partners = partner_tiles[0]
    count = pair_count[0]
    everyone = lax.all_gather(packed, "tile", axis=1, tiled=True)
    nearby = jnp.concatenate(
        [
            lax.dynamic_slice_in_dim(everyone, partners[slot] * gal_rows, gal_rows, 1)
            for slot in range(slots)
        ],
        axis=1,
    )

    def add_slot(slot, total):
        angles = lax.dynamic_slice_in_dim(pair_angle[0], slot * gal_rows, gal_rows, 1)
        bins = lax.dynamic_slice_in_dim(pair_bin[0], slot * gal_rows, gal_rows, 1)
        source = lax.dynamic_slice_in_dim(nearby, slot * gal_rows, gal_rows, 1)
        live = (slot < count).astype(jnp.float32)
        return total + slot_terms(angles, bins, source, live)

    empty = jnp.zeros((centres, NR, 2, NM), jnp.float32)
    tables = lax.fori_loop(0, slots, add_slot, empty)
    outgoing = tables.astype(jnp.bfloat16).reshape(zbins, gal_rows, NR * 2 * NM)
    arrived = lax.all_to_all(outgoing, "zbin", split_axis=0, concat_axis=0, tiled=True).reshape(
        zbins, gal_rows, NR, 2, NM
    )
    parts = rotate(arrived, packed)
    summed = lax.psum_scatter(products(parts, NM), "tile", scatter_dimension=0, tiled=True)
    return (summed * (tiles * GAL) ** (-0.5))[None]


def solution(mesh):
    return jax.shard_map(
        per_device,
        mesh=mesh,
        in_specs=(
            P("zbin", None, "tile"),
            P("zbin", "tile"),
            P("tile", None),
            P("tile"),
            P("zbin", "tile", None),
            P("zbin", "tile", None),
        ),
        out_specs=P("zbin", "tile", None),
        check_vma=False,
    )
```

profile of v0, /device:TPU:1, one launch (start us, length us, event | category | flops | bytes accessed | tf_op | source)
XLA Modules:
  0.0 631.2 jit_solution(4237256746885288594)
XLA Ops:
  11.2 40.5 %all-gather = f32[32,32,3]{1,2,0:T(4,128)S(1)} all-gather(f32[1,32,3]{1,2,0:T(4,128)S(1)} %maximum_bitcast_fusion), channel_id=1, replica_groups=mesh['tile'=32,'zbin'=8] {'tile'}, dimensions={0}, use_global_device_ids=true | all-gather | bytes 12672 | tf_op jit(solution)/shard_map/all_gather | solution.py:61
  53.0 76.8 %while.14 = (s32[]{:T(128)}, f32[256,24,2,32]{3,1,2,0:T(8,128)}, s32[1,256,128]{2,1,0:T(8,128)}, f32[3,128]{1,0:T(4,128)S(1)}, s32[]{:T(128)}, /*index=5*/f32[1,...) while((s32[]{:T(128)}, f32[256,24,2,32]{3,1,2,0:T(8,128)}, ...), condition=%wide.region_1.0_spmd.clone, body=%wide.region_0.0_spmd.clone.sunk | while | flops 29556808 | bytes 10160471 | solution.py:78
  58.2 6.5 %copy.31 = bf16[256,32,2,32]{3,1,2,0:T(8,128)(2,1)} copy(bf16[256,32,2,32]{0,3,2,1:T(8,128)(2,1)S(1)} %pad_maximum_fusion.4) | data formatting | bytes 2097152 | tf_op jit(solution)/shard_map/while/body/eval_jaxpr/stack | solution.py:21
  64.8 5.9 select_add_fusion.2
  76.0 6.5 %copy.31 = bf16[256,32,2,32]{3,1,2,0:T(8,128)(2,1)} copy(bf16[256,32,2,32]{0,3,2,1:T(8,128)(2,1)S(1)} %pad_maximum_fusion.4) | data formatting | bytes 2097152 | tf_op jit(solution)/shard_map/while/body/eval_jaxpr/stack | solution.py:21
  82.6 7.8 %select_add_fusion.2 = f32[256,24,2,32]{3,1,2,0:T(8,128)} fusion(f32[256,24,2,32]{3,1,2,0:T(8,128)} %get-tuple-element.229, pred[]{:T(512)S(6)} %compare.3, bf16[256,32,2,32]{3,1,2,0:T(8,128)(2,1)} %copy.31, s32[256,32]{1,0:T(8,128)S(1)} %dynamic-slice_bitcast_fusion.9), kind=kOutput, calls=%fused_computation.clone.1 | convolution fusion | flops 26148864 | bytes 4227073 | tf_op jit(solution)/shard_map/while/body/eval_jaxpr/ijb,ijpn->ibpn/dot_general | solution.py:24
  95.7 6.5 %copy.31 = bf16[256,32,2,32]{3,1,2,0:T(8,128)(2,1)} copy(bf16[256,32,2,32]{0,3,2,1:T(8,128)(2,1)S(1)} %pad_maximum_fusion.4) | data formatting | bytes 2097152 | tf_op jit(solution)/shard_map/while/body/eval_jaxpr/stack | solution.py:21
  102.3 7.8 %select_add_fusion.2 = f32[256,24,2,32]{3,1,2,0:T(8,128)} fusion(f32[256,24,2,32]{3,1,2,0:T(8,128)} %get-tuple-element.229, pred[]{:T(512)S(6)} %compare.3, bf16[256,32,2,32]{3,1,2,0:T(8,128)(2,1)} %copy.31, s32[256,32]{1,0:T(8,128)S(1)} %dynamic-slice_bitcast_fusion.9), kind=kOutput, calls=%fused_computation.clone.1 | convolution fusion | flops 26148864 | bytes 4227073 | tf_op jit(solution)/shard_map/while/body/eval_jaxpr/ijb,ijpn->ibpn/dot_general | solution.py:24
  115.3 6.5 %copy.31 = bf16[256,32,2,32]{3,1,2,0:T(8,128)(2,1)} copy(bf16[256,32,2,32]{0,3,2,1:T(8,128)(2,1)S(1)} %pad_maximum_fusion.4) | data formatting | bytes 2097152 | tf_op jit(solution)/shard_map/while/body/eval_jaxpr/stack | solution.py:21
  121.9 7.8 %select_add_fusion.2 = f32[256,24,2,32]{3,1,2,0:T(8,128)} fusion(f32[256,24,2,32]{3,1,2,0:T(8,128)} %get-tuple-element.229, pred[]{:T(512)S(6)} %compare.3, bf16[256,32,2,32]{3,1,2,0:T(8,128)(2,1)} %copy.31, s32[256,32]{1,0:T(8,128)S(1)} %dynamic-slice_bitcast_fusion.9), kind=kOutput, calls=%fused_computation.clone.1 | convolution fusion | flops 26148864 | bytes 4227073 | tf_op jit(solution)/shard_map/while/body/eval_jaxpr/ijb,ijpn->ibpn/dot_general | solution.py:24
  140.0 17.4 %all-to-all-start = ((bf16[8,32,1536]{2,1,0:T(8,128)(2,1)}), bf16[8,32,1536]{2,1,0:T(8,128)(2,1)}, u32[]{:S(2)}, u32[]{:S(2)}) async-start(bf16[8,32,1536]{2,1,0:T(8,128)(2,1)} %reshape.96), calls=%async_computation | async-start | bytes 1572864 | tf_op jit(solution)/shard_map/all_to_all | solution.py:80
  157.4 12.4 %all-to-all-done = bf16[8,32,1536]{2,1,0:T(8,128)(2,1)} async-done(((bf16[8,32,1536]{2,1,0:T(8,128)(2,1)}), bf16[8,32,1536]{2,1,0:T(8,128)(2,1)}, u32[]{:S(2)}, u32[]{:S(2)}) %all-to-all-start) | async-done | bytes 786464 | tf_op jit(solution)/shard_map/all_to_all | solution.py:80
  169.8 7.0 %reshape.87 = bf16[8,32,24,2,32]{4,3,2,1,0:T(2,128)(2,1)S(1)} reshape(bf16[8,32,1536]{2,1,0:T(8,128)(2,1)} %all-to-all-done) | data formatting | bytes 1572864 | tf_op jit(solution)/shard_map/reshape | solution.py:80
  176.9 6.1 fusion.35
  182.9 7.5 %copy.28 = bf16[8,32,24,1,32]{1,2,0,4,3:T(8,128)(2,1)S(1)} copy(bf16[8,32,24,1,32]{4,3,2,1,0:T(2,128)(2,1)} %get-tuple-element.160) | data formatting | bytes 786432
  190.5 7.5 %copy.29 = bf16[8,32,24,1,32]{1,2,0,4,3:T(8,128)(2,1)S(1)} copy(bf16[8,32,24,1,32]{4,3,2,1,0:T(2,128)(2,1)} %get-tuple-element.159) | data formatting | bytes 786432
  198.0 10.2 %fusion.28 = f32[32,8,24,8,24]{4,2,3,1,0:T(8,128)} fusion(bf16[8,32,24,1,32]{1,2,0,4,3:T(8,128)(2,1)S(1)} %copy.28, bf16[8,32,24,1,32]{1,2,0,4,3:T(8,128)(2,1)S(1)} %copy.29, f32[32]{0:T(128)S(1)} %get-tuple-element.166, f32[32]{0:T(128)S(1)} %get-tuple-element.165, f32[32]{0:T(128)S(1)} %bitcast.102), kind=kOutput, calls=%fused_computation.44 | convolution fusion | flops 76873728 | bytes 5505408 | tf_op jit(solution)/shard_map/zibn,yicn->nzbyc/dot_general | solution.py:42
  208.2 10.0 %fusion.26 = f32[32,8,24,8,24]{4,2,3,1,0:T(8,128)} fusion(bf16[8,32,24,1,32]{1,2,0,4,3:T(8,128)(2,1)S(1)} %copy.28, bf16[8,32,24,1,32]{1,2,0,4,3:T(8,128)(2,1)S(1)} %copy.29, f32[32]{0:T(128)S(1)} %get-tuple-element.166, f32[32]{0:T(128)S(1)} %get-tuple-element.165, f32[32]{0:T(128)S(1)} %bitcast.103), kind=kOutput, calls=%fused_computation.42 | convolution fusion | flops 76873728 | bytes 5505408 | tf_op jit(solution)/shard_map/zibn,yicn->nzbyc/dot_general | solution.py:45
  218.2 16.4 %add_bitcast_fusion = f32[32,1,8,24,8,24]{5,3,4,2,0,1:T(8,128)} fusion(f32[32,8,24,8,24]{4,2,3,1,0:T(8,128)} %fusion.28, bf16[8,32,24,1,32]{1,2,0,4,3:T(8,128)(2,1)S(1)} %copy.29, bf16[8,32,24,1,32]{1,2,0,4,3:T(8,128)(2,1)S(1)} %copy.28, f32[32]{0:T(128)S(1)} %get-tuple-element.166, f32[32]{0:T(128)S(1)} %get-tuple-element.165, f32[32]{0:T(128)S(1)} %bitcast.104), kind=kOutput, calls=%fused_computation.27 | convolution fusion | flops 78053376 | bytes 10224000 | tf_op jit(solution)/shard_map/zibn,yicn->nzbyc/dot_general | solution.py:44
  234.6 16.3 %subtract_bitcast_fusion = f32[32,1,8,24,8,24]{5,3,4,2,0,1:T(8,128)} fusion(f32[32,8,24,8,24]{4,2,3,1,0:T(8,128)} %fusion.26, bf16[8,32,24,1,32]{1,2,0,4,3:T(8,128)(2,1)S(1)} %copy.29, bf16[8,32,24,1,32]{1,2,0,4,3:T(8,128)(2,1)S(1)} %copy.28, f32[32]{0:T(128)S(1)} %get-tuple-element.166, f32[32]{0:T(128)S(1)} %get-tuple-element.165, f32[32]{0:T(128)S(1)} %bitcast.105), kind=kOutput, calls=%fused_computation.26 | convolution fusion | flops 78053376 | bytes 10224000 | tf_op jit(solution)/shard_map/zibn,yicn->nzbyc/dot_general | solution.py:47
  251.0 37.0 %pad_maximum_fusion.1 = f32[32,2,8,24,8,24]{5,3,4,2,0,1:T(8,128)} fusion(f32[32,1,8,24,8,24]{5,3,4,2,0,1:T(8,128)} %subtract_bitcast_fusion, f32[32,1,8,24,8,24]{5,3,4,2,0,1:T(8,128)} %add_bitcast_fusion), kind=kLoop, calls=%fused_computation.25 | loop fusion | flops 2359296 | bytes 18874368 | tf_op jit(solution)/shard_map/stack | solution.py:49
  288.0 41.3 %copy.20 = f32[32,2,8,24,8,24]{5,4,3,2,1,0:T(8,128)} copy(f32[32,2,8,24,8,24]{5,3,4,2,0,1:T(8,128)} %pad_maximum_fusion.1) | data formatting | bytes 18874368 | tf_op jit(solution)/shard_map/stack | solution.py:49
  329.2 70.9 %reshape.88 = f32[32,73728]{1,0:T(8,128)} reshape(f32[32,2,8,24,8,24]{5,4,3,2,1,0:T(8,128)} %copy.20) | data formatting | bytes 18874368 | tf_op jit(solution)/shard_map/reshape | solution.py:49
  401.4 219.7 %all-reduce.3.cloned.1.call-done = f32[32,73728]{1,0:T(8,128)} async-done(((f32[32,73728]{1,0:T(8,128)}), f32[32,73728]{1,0:T(8,128)}) %all-reduce.3.cloned.1.call-update) | async-done | bytes 9437200
  (58 shorter events, 36.8 us)
Async XLA Ops:
  58.2 6.5 %copy-start = (s32[1,256,128]{2,1,0:T(8,128)S(1)}, s32[1,256,128]{2,1,0:T(8,128)}, u32[]{:S(2)}) copy-start(s32[1,256,128]{2,1,0:T(8,128)} %get-tuple-element.240) | copy-start | bytes 393220 | tf_op jit(solution)/shard_map/while
  76.0 6.5 %copy-start = (s32[1,256,128]{2,1,0:T(8,128)S(1)}, s32[1,256,128]{2,1,0:T(8,128)}, u32[]{:S(2)}) copy-start(s32[1,256,128]{2,1,0:T(8,128)} %get-tuple-element.240) | copy-start | bytes 393220 | tf_op jit(solution)/shard_map/while
  95.7 6.5 %copy-start = (s32[1,256,128]{2,1,0:T(8,128)S(1)}, s32[1,256,128]{2,1,0:T(8,128)}, u32[]{:S(2)}) copy-start(s32[1,256,128]{2,1,0:T(8,128)} %get-tuple-element.240) | copy-start | bytes 393220 | tf_op jit(solution)/shard_map/while
  115.3 6.5 %copy-start = (s32[1,256,128]{2,1,0:T(8,128)S(1)}, s32[1,256,128]{2,1,0:T(8,128)}, u32[]{:S(2)}) copy-start(s32[1,256,128]{2,1,0:T(8,128)} %get-tuple-element.240) | copy-start | bytes 393220 | tf_op jit(solution)/shard_map/while
  136.2 21.2 %copy-start.2 = (f32[1,2,32]{2,1,0:T(2,128)S(1)}, f32[1,2,32]{2,1,0:T(2,128)}, u32[]{:S(2)}) copy-start(f32[1,2,32]{2,1,0:T(2,128)} %param.8) | copy-start | bytes 772
  140.0 29.8 %all-to-all-start = ((bf16[8,32,1536]{2,1,0:T(8,128)(2,1)}), bf16[8,32,1536]{2,1,0:T(8,128)(2,1)}, u32[]{:S(2)}, u32[]{:S(2)}) async-start(bf16[8,32,1536]{2,1,0:T(8,128)(2,1)} %reshape.96), calls=%async_computation | async-start | bytes 1572864 | tf_op jit(solution)/shard_map/all_to_all | solution.py:80
  157.4 463.7 %all-reduce.3.cloned.1.call-start = ((), (), s32[]{:S(2)}) async-start(), calls=%async_computation.1 | async-start | bytes 18874368
  190.5 7.6 %copy-start.1 = (f32[1,32]{1,0:T(1,128)S(1)}, f32[1,32]{1,0:T(1,128)}, u32[]{:S(2)}) copy-start(f32[1,32]{1,0:T(1,128)} %param.9) | copy-start | bytes 388
  400.1 0.7 copy-start.3
Sparse Core Ops, SparseCore 0:
  400.3 220.8 all-reduce.2
where the time goes:
time: 632 us; the launch traced here: 631 us
  waiting for transfers between devices  232 us (37%)
  local copies, waits for them, and re-layouts  178 us (28%)
  matrix products  82.3 us (13%)
  other arithmetic  62.1 us (10%)
  blocking collectives  40.5 us (6%)
  starting transfers between devices  17.4 us (3%)
  between operations  16 us (3%)
    unnamed x2, waiting for transfers between devices  220 us
    reshape x1, local copies, waits for them, and re-layouts, products(): jnp.stack([real_out, imag_out], axis=1).reshape(number, 2 * legs * legs)  70.9 us
    another operation x1, local copies, waits for them, and re-layouts, products(): jnp.stack([real_out, imag_out], axis=1).reshape(number, 2 * legs * legs)  41.3 us
    all_gather x1, blocking collectives, per_device(): everyone = lax.all_gather(packed, 'tile', axis=1, tiled=True)  40.5 us
    another operation x1, other arithmetic, products(): jnp.stack([real_out, imag_out], axis=1).reshape(number, 2 * legs * legs)  37 us
    dot_general x4, matrix products, slot_terms(): jnp.einsum('ijb,ijpn->ibpn', onehot, terms, preferred_element_type=jnp.fl...  29.4 us
    another operation x4, local copies, waits for them, and re-layouts, slot_terms(): terms = jnp.stack([real_part, imag_part], axis=2).astype(jnp.bfloat16)  25.9 us
    unnamed x11, local copies, waits for them, and re-layouts  17.4 us
  transfers between devices with their start and end apart: 2, of which 2 were waited for; matrix products, arithmetic and copies ran while one was open for 0% of the time, Pallas kernels for 0%

commit v1 on v0

v1 whole, which is shorter than its diff:
```python
import jax
import jax.numpy as jnp
from jax import lax
from jax.experimental import pallas as pl
from jax.experimental.pallas import tpu as pltpu
from jax.sharding import PartitionSpec as P

GAL = 32
NM = 32
NR = 24
ZB = 8
TILES = 32
YS = 4
ZS = TILES // YS
LANES = 128
HALF = 16
LEGS = ZB * NR
WIDE = 2 * LEGS
MESH = pl.DeviceIdType.MESH


def sine_cosine(phi):
    half = phi * 0.5
    sq = half * half
    sin_h = -2.5052108385e-08
    for coefficient in (2.7557319224e-06, -1.9841269841e-04, 8.3333333333e-03, -1.6666666667e-01):
        sin_h = sin_h * sq + coefficient
    sin_h = half + half * (sq * sin_h)
    cos_h = 2.0876756988e-09
    for coefficient in (-2.7557319224e-07, 2.4801587302e-05, -1.3888888889e-03, 4.1666666667e-02, -0.5):
        cos_h = cos_h * sq + coefficient
    cos_h = 1.0 + sq * cos_h
    return 2.0 * sin_h * cos_h, 1.0 - 2.0 * sin_h * sin_h


def kernel(
    shear, weight, partners, count, bins_in, angles_in, out,
    every, near, phi, bins, start, rot_c, rot_s, grid0, grid1, grid2, send, got,
    wide_re, wide_im, block_a, block_b,
    own_sem, every_send, every_recv, raw_send, raw_recv, near_send, near_recv, tab_send, tab_recv,
):
    me_t = lax.axis_index("tile")
    me_z = lax.axis_index("zbin")
    at_z, at_y = me_t // YS, me_t % YS

    def tile_at(slot):
        return ((at_z + slot // YS) % ZS) * YS + (at_y + slot % YS) % YS

    def tile_from(slot):
        return ((at_z + ZS - slot // YS) % ZS) * YS + (at_y + YS - slot % YS) % YS

    def bin_at(step):
        return (me_z + step) % ZB

    def rows_of(centre_bin):
        return pl.ds(pl.multiple_of(centre_bin * GAL, GAL), GAL)

    own_angles = pltpu.make_async_copy(angles_in.at[0, rows_of(me_z)], phi.at[me_z], own_sem.at[0])
    own_bins = pltpu.make_async_copy(bins_in.at[0, rows_of(me_z)], bins.at[me_z], own_sem.at[1])
    own_angles.start()
    own_bins.start()
    scaled = shear[0] * weight[...]
    every[0] = jnp.concatenate([scaled] * (LANES // GAL), axis=1)

    barrier = pltpu.get_barrier_semaphore()

    @pl.loop(1, TILES)
    def _(slot):
        pl.semaphore_signal(barrier, inc=1, device_id={"tile": tile_at(slot)}, device_id_type=MESH)

    @pl.loop(1, ZB)
    def _(step):
        pl.semaphore_signal(barrier, inc=1, device_id={"zbin": bin_at(step)}, device_id_type=MESH)

    pl.semaphore_wait(barrier, TILES + ZB - 2)

    def every_copy(slot):
        return pltpu.make_async_remote_copy(
            src_ref=every.at[0], dst_ref=every.at[slot],
            send_sem=every_send.at[slot], recv_sem=every_recv.at[slot],
            device_id={"tile": tile_at(slot)}, device_id_type=MESH,
        )

    def raw_copy(step, kind, source, target):
        to = bin_at(step)
        return pltpu.make_async_remote_copy(
            src_ref=source.at[0, rows_of(to)], dst_ref=target.at[me_z],
            send_sem=raw_send.at[kind, step], recv_sem=raw_recv.at[kind, step],
            device_id={"zbin": to}, device_id_type=MESH,
        )

    def near_copy(step):
        return pltpu.make_async_remote_copy(
            src_ref=near.at[me_z], dst_ref=near.at[me_z],
            send_sem=near_send.at[step], recv_sem=near_recv.at[step],
            device_id={"zbin": bin_at(step)}, device_id_type=MESH,
        )

    @pl.loop(1, TILES)
    def _(slot):
        every_copy(slot).start()

    @pl.loop(1, ZB)
    def _(step):
        raw_copy(step, 0, angles_in, phi).start()
        raw_copy(step, 1, bins_in, bins).start()

    own_angles.wait()
    own_bins.wait()

    @pl.loop(1, TILES)
    def _(slot):
        every_copy(slot).wait_recv()

    lane = lax.broadcasted_iota(jnp.int32, (2, LANES), 1)
    place = lane // GAL
    wanted = jnp.full((2, LANES), partners[0, 0])
    for slot in range(1, LANES // GAL):
        wanted = jnp.where(place == slot, partners[0, slot], wanted)
    wanted = jnp.where(place < count[0], wanted, -1)
    picked = jnp.zeros((2, LANES), jnp.float32)
    for slot in range(TILES):
        picked = picked + jnp.where(wanted == tile_from(slot), every[slot], 0.0)
    near[me_z] = picked

    @pl.loop(1, ZB)
    def _(step):
        near_copy(step).start()

    @pl.loop(1, ZB)
    def _(step):
        raw_copy(step, 0, angles_in, phi).wait_recv()
        raw_copy(step, 1, bins_in, bins).wait_recv()

    @pl.loop(0, ZB)
    def _(z):
        sine, cosine = sine_cosine(phi[z])
        phi[z] = cosine
        rot_s[z] = sine

    @pl.loop(1, ZB)
    def _(step):
        near_copy(step).wait_recv()

    @pl.loop(0, ZB)
    def _(z):
        cosine, sine = phi[z], rot_s[z]
        first = jnp.broadcast_to(near[z, 0:1, :], (GAL, LANES))
        second = jnp.broadcast_to(near[z, 1:2, :], (GAL, LANES))
        twice = 2.0 * cosine
        base = pl.multiple_of(z * 16 * GAL, 16 * GAL)
        old_re, old_im = first, second
        new_re = first * cosine + second * sine
        new_im = second * cosine - first * sine
        for n in range(8):
            start[pl.ds(base + n * GAL, GAL), :] = old_re
            start[pl.ds(base + (8 + n) * GAL, GAL), :] = old_im
            old_re, new_re = new_re, twice * new_re - old_re
            old_im, new_im = new_im, twice * new_im - old_im
        for _ in range(3):
            cosine, sine = 1.0 - 2.0 * sine * sine, 2.0 * sine * cosine
        rot_c[z] = cosine
        rot_s[z] = sine

    level = lax.broadcasted_iota(jnp.int32, (NR, LANES), 0)
    blank = jnp.zeros((NR, LANES), jnp.float32)

    def centre_table(i, local):
        parts = []
        for pair in range(ZB // 2):
            terms, hits = [], []
            for z in (2 * pair, 2 * pair + 1):
                base = z * 16 * GAL
                re = [start[pl.ds(base + i, 8, stride=GAL), :]]
                im = [start[pl.ds(base + 8 * GAL + i, 8, stride=GAL), :]]
                cosine = jnp.broadcast_to(rot_c[z, pl.ds(i, 1), :], (8, LANES))
                sine = jnp.broadcast_to(rot_s[z, pl.ds(i, 1), :], (8, LANES))
                twice = cosine + cosine
                re.append(re[0] * cosine + im[0] * sine)
                im.append(im[0] * cosine - re[0] * sine)
                for _ in range(2):
                    re.append(twice * re[-1] - re[-2])
                    im.append(twice * im[-1] - im[-2])
                terms.append(jnp.concatenate(re + im, axis=0).astype(jnp.bfloat16))
                row = jnp.broadcast_to(bins[z, pl.ds(i, 1), :], (NR, LANES))
                hits.append(jnp.where(row == level, 1.0, 0.0))
            onehot = jnp.concatenate(
                [jnp.concatenate([hits[0], blank], axis=1), jnp.concatenate([blank, hits[1]], axis=1)],
                axis=0,
            ).astype(jnp.bfloat16)
            parts.append(
                lax.dot_general(
                    jnp.concatenate(terms, axis=1), onehot, (((1,), (1,)), ((), ())),
                    preferred_element_type=jnp.float32,
                )
            )
        table = jnp.concatenate(parts, axis=1)
        rows = pl.ds(local, NM, stride=HALF)
        grid0[rows, :] = table[:NM, :LANES]
        grid1[rows, :] = jnp.concatenate([table[:NM, LANES:], table[NM:, LANES:]], axis=1)
        grid2[rows, :] = table[NM:, :LANES]

    def table_copy(half, slot):
        return pltpu.make_async_remote_copy(
            src_ref=send.at[half, tile_at(slot)],
            dst_ref=got.at[pl.ds(pl.multiple_of(slot * GAL + half * HALF, HALF), HALF), :],
            send_sem=tab_send.at[half, slot], recv_sem=tab_recv.at[half, slot],
            device_id={"tile": tile_at(slot)}, device_id_type=MESH,
        )

    for half in range(2):
        @pl.loop(0, HALF, unroll=2)
        def _(local):
            centre_table(half * HALF + local, local)

        @pl.loop(0, NM, unroll=4)
        def _(n):
            rows = pl.ds(pl.multiple_of(n * HALF, HALF), HALF)
            send[half, n, :, 0:LANES] = grid0[rows, :].astype(jnp.bfloat16)
            send[half, n, :, LANES:2 * LANES] = grid1[rows, :].astype(jnp.bfloat16)
            send[half, n, :, 2 * LANES:] = grid2[rows, :].astype(jnp.bfloat16)

        @pl.loop(1, TILES)
        def _(slot):
            table_copy(half, slot).start()

        got[half * HALF:(half + 1) * HALF, :] = send[half, me_t]

    lane = lax.broadcasted_iota(jnp.int32, (2, LANES), 1)
    wide_re[...] = jnp.zeros_like(wide_re)
    wide_im[...] = jnp.zeros_like(wide_im)
    group = 8
    for g in range(TILES // group):
        @pl.loop(max(g * group, 1), (g + 1) * group)
        def _(slot):
            for half in range(2):
                table_copy(half, slot).wait_recv()

        block = got[g * group * GAL:(g + 1) * group * GAL, :]
        turned = block.T.astype(jnp.float32)
        scales = []
        for quad in range(group * GAL // LANES):
            first = g * group + quad * (LANES // GAL)
            row = every[first]
            for k in range(1, LANES // GAL):
                row = jnp.where(lane // GAL == k, every[first + k], row)
            scales.append(row)
        scales = jnp.concatenate(scales, axis=1)
        first, second = scales[0:1], scales[1:2]
        real_in = turned[:LEGS]
        imag_in = jnp.concatenate([turned[WIDE - LANES:], turned[LEGS:WIDE - LANES]], axis=0)
        upper_re = (first * real_in - second * imag_in).astype(jnp.bfloat16)
        upper_im = (first * imag_in + second * real_in).astype(jnp.bfloat16)
        wide_re[...] += jnp.dot(upper_re, block, preferred_element_type=jnp.float32)
        wide_im[...] += jnp.dot(upper_im, block, preferred_element_type=jnp.float32)

    scale = float(TILES * GAL) ** -0.5
    low = lax.broadcasted_iota(jnp.int32, (LEGS // 2, LANES), 1) < LANES // 2
    for part in range(2):
        if part == 0:
            whole = wide_re[:, :LANES] + wide_im[:, 2 * LANES:]
            rest = wide_re[:, LANES:2 * LANES] + pltpu.roll(wide_im[:, LANES:2 * LANES], LANES // 2, 1)
        else:
            whole = wide_im[:, :LANES] - wide_re[:, 2 * LANES:]
            rest = wide_im[:, LANES:2 * LANES] - pltpu.roll(wide_re[:, LANES:2 * LANES], LANES // 2, 1)
        block_a[...] = whole * scale
        block_b[...] = rest * scale
        base = part * LEGS * LEGS // LANES
        even_a = block_a[pl.ds(0, LEGS // 2, stride=2), :]
        odd_a = pltpu.roll(block_a[pl.ds(1, LEGS // 2, stride=2), :], LANES // 2, 1)
        even_b = block_b[pl.ds(0, LEGS // 2, stride=2), :]
        odd_b = pltpu.roll(block_b[pl.ds(1, LEGS // 2, stride=2), :], LANES // 2, 1)
        out[pl.ds(base, LEGS // 2, stride=3), :] = even_a
        out[pl.ds(base + 1, LEGS // 2, stride=3), :] = jnp.where(low, even_b, odd_a)
        out[pl.ds(base + 2, LEGS // 2, stride=3), :] = jnp.where(low, odd_a, odd_b)

    @pl.loop(1, TILES)
    def _(slot):
        every_copy(slot).wait_send()
        for half in range(2):
            table_copy(half, slot).wait_send()

    @pl.loop(1, ZB)
    def _(step):
        raw_copy(step, 0, angles_in, phi).wait_send()
        raw_copy(step, 1, bins_in, bins).wait_send()
        near_copy(step).wait_send()


def per_device(shear, weight, partner_tiles, pair_count, pair_bin, pair_angle):
    vmem = pl.BlockSpec(memory_space=pltpu.VMEM)
    smem = pl.BlockSpec(memory_space=pltpu.SMEM)
    anywhere = pl.BlockSpec(memory_space=pl.ANY)
    f32, bf16 = jnp.float32, jnp.bfloat16
    flat = pl.pallas_call(
        kernel,
        out_shape=jax.ShapeDtypeStruct((2 * LEGS * LEGS // LANES, LANES), f32),
        in_specs=[vmem, vmem, smem, smem, anywhere, anywhere],
        out_specs=vmem,
        scratch_shapes=[
            pltpu.VMEM((TILES, 2, LANES), f32),
            pltpu.VMEM((ZB, 2, LANES), f32),
            pltpu.VMEM((ZB, GAL, LANES), f32),
            pltpu.VMEM((ZB, GAL, LANES), jnp.int32),
            pltpu.VMEM((ZB * 16 * GAL, LANES), f32),
            pltpu.VMEM((ZB, GAL, LANES), f32),
            pltpu.VMEM((ZB, GAL, LANES), f32),
            pltpu.VMEM((NM * HALF, LANES), f32),
            pltpu.VMEM((NM * HALF, LANES), f32),
            pltpu.VMEM((NM * HALF, LANES), f32),
            pltpu.VMEM((2, NM, HALF, WIDE), bf16),
            pltpu.VMEM((TILES * GAL, WIDE), bf16),
            pltpu.VMEM((LEGS, WIDE), f32),
            pltpu.VMEM((LEGS, WIDE), f32),
            pltpu.VMEM((LEGS, LANES), f32),
            pltpu.VMEM((LEGS, LANES), f32),
            pltpu.SemaphoreType.DMA((2,)),
            pltpu.SemaphoreType.DMA((TILES,)),
            pltpu.SemaphoreType.DMA((TILES,)),
            pltpu.SemaphoreType.DMA((2, ZB)),
            pltpu.SemaphoreType.DMA((2, ZB)),
            pltpu.SemaphoreType.DMA((ZB,)),
            pltpu.SemaphoreType.DMA((ZB,)),
            pltpu.SemaphoreType.DMA((2, TILES)),
            pltpu.SemaphoreType.DMA((2, TILES)),
        ],
        compiler_params=pltpu.CompilerParams(
            collective_id=0, has_side_effects=True, vmem_limit_bytes=40 * 1024 * 1024
        ),
        cost_estimate=pl.CostEstimate(flops=800_000_000, bytes_accessed=2_000_000, transcendentals=0),
        name="shear_triples",
    )(shear, weight, partner_tiles, pair_count, pair_bin, pair_angle)
    return flat.reshape(1, 1, 2 * LEGS * LEGS)


def solution(mesh):
    return jax.shard_map(
        per_device,
        mesh=mesh,
        in_specs=(
            P("zbin", None, "tile"),
            P("zbin", "tile"),
            P("tile", None),
            P("tile"),
            P("zbin", "tile", None),
            P("zbin", "tile", None),
        ),
        out_specs=P("zbin", "tile", None),
        check_vma=False,
    )
```

time: 632 us -> 53.4 us (0.08)
  waiting for transfers between devices: 232 us -> 0 us
  local copies, waits for them, and re-layouts: 178 us -> 3.18 us
  matrix products: 82.3 us -> 0 us
  other arithmetic: 62.1 us -> 0 us
  Pallas kernels: 0 us -> 49.4 us
  blocking collectives: 40.5 us -> 0 us
  starting transfers between devices: 17.4 us -> 0 us
  between operations: 16 us -> 0.72 us
    unnamed x2 -> x0, waiting for transfers between devices: 220 us -> none
    reshape x4 -> x0, local copies, waits for them, and re-layouts: 85 us -> none  [the longest x1 70.9 us: products(): jnp.stack([real_out, imag_out], axis=1).reshape(number, 2 * legs * legs)]
    dot_general x8 -> x0, matrix products: 82.3 us -> none  [the longest x4 29.4 us: slot_terms(): jnp.einsum('ijb,ijpn->ibpn', onehot, terms, preferred_element_type=jnp.fl...]
    another operation x5 -> x0, local copies, waits for them, and re-layouts: 67.2 us -> none  [the longest x1 41.3 us: products(): jnp.stack([real_out, imag_out], axis=1).reshape(number, 2 * legs * legs)]
    another operation x9 -> x0, other arithmetic: 54.8 us -> none  [the longest x1 37 us: products(): jnp.stack([real_out, imag_out], axis=1).reshape(number, 2 * legs * legs)]
    pallas_call x0 -> x1, Pallas kernels: none -> 49.4 us  [per_device(): pl.pallas_call(kernel, out_shape=jax.ShapeDtypeStruct((2 * LEGS * LEGS //...]
    all_gather x1 -> x0, blocking collectives: 40.5 us -> none  [per_device(): everyone = lax.all_gather(packed, 'tile', axis=1, tiled=True)]
    all_to_all x1 -> x0, starting transfers between devices: 17.4 us -> none  [per_device(): lax.all_to_all(outgoing, 'zbin', split_axis=0, concat_axis=0, tiled=True)]
  transfers between devices with their start and end apart: 2 -> 0, of which waited for: 2 -> 0; matrix products, arithmetic and copies ran while one was open for 0% -> 0% of each run, Pallas kernels for 0% -> 0%
where the time goes in v1:
time: 53.4 us; the launch traced here: 53.3 us
  Pallas kernels  49.4 us (93%)
  local copies, waits for them, and re-layouts  3.18 us (6%)
  between operations  0.72 us (1%)
    pallas_call x1, Pallas kernels, per_device(): pl.pallas_call(kernel, out_shape=jax.ShapeDtypeStruct((2 * LEGS * LEGS //...  49.4 us
    unnamed x11, local copies, waits for them, and re-layouts  3.18 us

profile of v1, /device:TPU:1, one launch (start us, length us, event | category | flops | bytes accessed | tf_op | source)
XLA Modules:
  0.0 53.3 jit_solution(16394242793536830999)
XLA Ops:
  0.0 0.0 copy-start.3
  0.0 0.0 copy-start.2
  0.7 0.0 copy-done.3
  0.7 0.0 copy-done.2
  0.7 0.0 copy-start
  0.7 0.9 %copy-done = s32[1,256,128]{2,1,0:T(8,128)S(1)} copy-done((s32[1,256,128]{2,1,0:T(8,128)S(1)}, s32[1,256,128]{2,1,0:T(8,128)}, u32[]{:S(2)}) %copy-start) | copy-done | bytes 131096
  1.6 0.0 copy-start.1
  1.6 0.9 %copy-done.1 = f32[1,256,128]{2,1,0:T(8,128)S(1)} copy-done((f32[1,256,128]{2,1,0:T(8,128)S(1)}, f32[1,256,128]{2,1,0:T(8,128)}, u32[]{:S(2)}) %copy-start.1) | copy-done | bytes 131096
  2.5 0.0 copy-start.4
  2.5 0.7 %copy-done.4 = s32[1,4]{1,0:T(1,128)S(1)} copy-done((s32[1,4]{1,0:T(1,128)S(1)}, s32[1,4]{1,0:T(1,128)}, u32[]{:S(2)}) %copy-start.4) | copy-done | bytes 40
  3.2 49.4 %shear_triples.1 = f32[576,128]{1,0:T(8,128)S(1)} custom-call(f32[1,2,32]{2,1,0:T(2,128)S(1)} %copy-done.2, f32[1,32]{1,0:T(1,128)S(1)} %copy-done.3, s32[1,4]{1,0:T(1,128)S(1)} %copy-done.4, s32[1]{0:T(128)S(6)} %copy.8.count, s32[1,256,128]{2,1,0:T(8,128)S(1)} %copy-done, f32[1,256,128]{2,1,0:T(8,128)S(1)} %copy-done.1), custom_call_target="tpu_custom_call" | custom-call | flops 800000000 | bytes 2000000 | tf_op jit(solution)/shard_map/shear_triples/pallas_call | solution.py:295
  52.5 0.7 %copy.9 = f32[1,1,73728]{2,1,0:T(1,128)} copy(f32[1,1,73728]{2,1,0:T(1,128)S(1)} %bitcast.1) | data formatting | bytes 589824
Async XLA Ops:
  0.0 0.7 %copy-start.3 = (f32[1,32]{1,0:T(1,128)S(1)}, f32[1,32]{1,0:T(1,128)}, u32[]{:S(2)}) copy-start(f32[1,32]{1,0:T(1,128)} %weight.1) | copy-start | bytes 388
  0.0 0.7 %copy-start.2 = (f32[1,2,32]{2,1,0:T(2,128)S(1)}, f32[1,2,32]{2,1,0:T(2,128)}, u32[]{:S(2)}) copy-start(f32[1,2,32]{2,1,0:T(2,128)} %shear.1) | copy-start | bytes 772
  0.7 0.9 %copy-start = (s32[1,256,128]{2,1,0:T(8,128)S(1)}, s32[1,256,128]{2,1,0:T(8,128)}, u32[]{:S(2)}) copy-start(s32[1,256,128]{2,1,0:T(8,128)} %bins_in.1) | copy-start | bytes 393220
  1.6 0.9 %copy-start.1 = (f32[1,256,128]{2,1,0:T(8,128)S(1)}, f32[1,256,128]{2,1,0:T(8,128)}, u32[]{:S(2)}) copy-start(f32[1,256,128]{2,1,0:T(8,128)} %angles_in.1) | copy-start | bytes 393220
  2.5 0.7 %copy-start.4 = (s32[1,4]{1,0:T(1,128)S(1)}, s32[1,4]{1,0:T(1,128)}, u32[]{:S(2)}) copy-start(s32[1,4]{1,0:T(1,128)} %partners.1) | copy-start | bytes 52

commit v2 on v1

--- a/solution.py
+++ b/solution.py
@@ -16,6 +16,7 @@
 HALF = 16
 LEGS = ZB * NR
 WIDE = 2 * LEGS
+OWN = TILES - 1
 MESH = pl.DeviceIdType.MESH
 
 
@@ -34,20 +35,26 @@
 
 
 def kernel(
-    shear, weight, partners, count, bins_in, angles_in, out,
-    every, near, phi, bins, start, rot_c, rot_s, grid0, grid1, grid2, send, got,
+    shear_in, weight_in, partners_in, count_in, bins_in, angles_in, out,
+    shear, weight, partners, count, every, near, phi, bins, start, rot_c, rot_s, grid0, grid1, grid2, send, got,
     wide_re, wide_im, block_a, block_b,
-    own_sem, every_send, every_recv, raw_send, raw_recv, near_send, near_recv, tab_send, tab_recv,
+    small_sem, own_sem, every_send, every_recv, raw_send, raw_recv, near_send, near_recv, tab_send, tab_recv,
 ):
     me_t = lax.axis_index("tile")
     me_z = lax.axis_index("zbin")
     at_z, at_y = me_t // YS, me_t % YS
 
+    def steps(slot):
+        k = slot // YS
+        return (ZS // 2 + (k + 1) // 2 * (1 - 2 * (k % 2))) % ZS, (slot + 1) % YS
+
     def tile_at(slot):
-        return ((at_z + slot // YS) % ZS) * YS + (at_y + slot % YS) % YS
+        z, y = steps(slot)
+        return ((at_z + z) % ZS) * YS + (at_y + y) % YS
 
     def tile_from(slot):
-        return ((at_z + ZS - slot // YS) % ZS) * YS + (at_y + YS - slot % YS) % YS
+        z, y = steps(slot)
+        return ((at_z + ZS - z) % ZS) * YS + (at_y + YS - y) % YS
 
     def bin_at(step):
         return (me_z + step) % ZB
@@ -55,16 +62,21 @@
     def rows_of(centre_bin):
         return pl.ds(pl.multiple_of(centre_bin * GAL, GAL), GAL)
 
+    small = [
+        pltpu.make_async_copy(shear_in, shear, small_sem.at[0]),
+        pltpu.make_async_copy(weight_in, weight, small_sem.at[1]),
+        pltpu.make_async_copy(partners_in, partners, small_sem.at[2]),
+        pltpu.make_async_copy(count_in, count, small_sem.at[3]),
+    ]
+    for copy in small:
+        copy.start()
     own_angles = pltpu.make_async_copy(angles_in.at[0, rows_of(me_z)], phi.at[me_z], own_sem.at[0])
     own_bins = pltpu.make_async_copy(bins_in.at[0, rows_of(me_z)], bins.at[me_z], own_sem.at[1])
     own_angles.start()
     own_bins.start()
-    scaled = shear[0] * weight[...]
-    every[0] = jnp.concatenate([scaled] * (LANES // GAL), axis=1)
-
     barrier = pltpu.get_barrier_semaphore()
 
-    @pl.loop(1, TILES)
+    @pl.loop(0, OWN)
     def _(slot):
         pl.semaphore_signal(barrier, inc=1, device_id={"tile": tile_at(slot)}, device_id_type=MESH)
 
@@ -72,11 +84,15 @@
     def _(step):
         pl.semaphore_signal(barrier, inc=1, device_id={"zbin": bin_at(step)}, device_id_type=MESH)
 
+    for copy in small:
+        copy.wait()
+    scaled = shear[0] * weight[...]
+    every[OWN] = jnp.concatenate([scaled] * (LANES // GAL), axis=1)
     pl.semaphore_wait(barrier, TILES + ZB - 2)
 
     def every_copy(slot):
         return pltpu.make_async_remote_copy(
-            src_ref=every.at[0], dst_ref=every.at[slot],
+            src_ref=every.at[OWN], dst_ref=every.at[slot],
             send_sem=every_send.at[slot], recv_sem=every_recv.at[slot],
             device_id={"tile": tile_at(slot)}, device_id_type=MESH,
         )
@@ -96,7 +112,7 @@
             device_id={"zbin": bin_at(step)}, device_id_type=MESH,
         )
 
-    @pl.loop(1, TILES)
+    @pl.loop(0, OWN)
     def _(slot):
         every_copy(slot).start()
 
@@ -108,7 +124,7 @@
     own_angles.wait()
     own_bins.wait()
 
-    @pl.loop(1, TILES)
+    @pl.loop(0, OWN)
     def _(slot):
         every_copy(slot).wait_recv()
 
@@ -117,7 +133,7 @@
     wanted = jnp.full((2, LANES), partners[0, 0])
     for slot in range(1, LANES // GAL):
         wanted = jnp.where(place == slot, partners[0, slot], wanted)
-    wanted = jnp.where(place < count[0], wanted, -1)
+    wanted = jnp.where(place < count[0, 0], wanted, -1)
     picked = jnp.zeros((2, LANES), jnp.float32)
     for slot in range(TILES):
         picked = picked + jnp.where(wanted == tile_from(slot), every[slot], 0.0)
@@ -220,18 +236,18 @@
             send[half, n, :, LANES:2 * LANES] = grid1[rows, :].astype(jnp.bfloat16)
             send[half, n, :, 2 * LANES:] = grid2[rows, :].astype(jnp.bfloat16)
 
-        @pl.loop(1, TILES)
+        @pl.loop(0, OWN)
         def _(slot):
             table_copy(half, slot).start()
 
-        got[half * HALF:(half + 1) * HALF, :] = send[half, me_t]
+        got[OWN * GAL + half * HALF:OWN * GAL + (half + 1) * HALF, :] = send[half, me_t]
 
     lane = lax.broadcasted_iota(jnp.int32, (2, LANES), 1)
     wide_re[...] = jnp.zeros_like(wide_re)
     wide_im[...] = jnp.zeros_like(wide_im)
     group = 8
     for g in range(TILES // group):
-        @pl.loop(max(g * group, 1), (g + 1) * group)
+        @pl.loop(g * group, min((g + 1) * group, OWN))
         def _(slot):
             for half in range(2):
                 table_copy(half, slot).wait_recv()
@@ -274,7 +290,7 @@
         out[pl.ds(base + 1, LEGS // 2, stride=3), :] = jnp.where(low, even_b, odd_a)
         out[pl.ds(base + 2, LEGS // 2, stride=3), :] = jnp.where(low, odd_a, odd_b)
 
-    @pl.loop(1, TILES)
+    @pl.loop(0, OWN)
     def _(slot):
         every_copy(slot).wait_send()
         for half in range(2):
@@ -289,15 +305,18 @@
 
 def per_device(shear, weight, partner_tiles, pair_count, pair_bin, pair_angle):
     vmem = pl.BlockSpec(memory_space=pltpu.VMEM)
-    smem = pl.BlockSpec(memory_space=pltpu.SMEM)
     anywhere = pl.BlockSpec(memory_space=pl.ANY)
     f32, bf16 = jnp.float32, jnp.bfloat16
     flat = pl.pallas_call(
         kernel,
-        out_shape=jax.ShapeDtypeStruct((2 * LEGS * LEGS // LANES, LANES), f32),
-        in_specs=[vmem, vmem, smem, smem, anywhere, anywhere],
+        out_shape=pltpu.VMEM((2 * LEGS * LEGS // LANES, LANES), f32),
+        in_specs=[anywhere] * 6,
         out_specs=vmem,
         scratch_shapes=[
+            pltpu.VMEM((1, 2, GAL), f32),
+            pltpu.VMEM((1, GAL), f32),
+            pltpu.SMEM((1, LANES // GAL), jnp.int32),
+            pltpu.SMEM((1, 1), jnp.int32),
             pltpu.VMEM((TILES, 2, LANES), f32),
             pltpu.VMEM((ZB, 2, LANES), f32),
             pltpu.VMEM((ZB, GAL, LANES), f32),
@@ -314,6 +333,7 @@
             pltpu.VMEM((LEGS, WIDE), f32),
             pltpu.VMEM((LEGS, LANES), f32),
             pltpu.VMEM((LEGS, LANES), f32),
+            pltpu.SemaphoreType.DMA((4,)),
             pltpu.SemaphoreType.DMA((2,)),
             pltpu.SemaphoreType.DMA((TILES,)),
             pltpu.SemaphoreType.DMA((TILES,)),
@@ -325,11 +345,11 @@
             pltpu.SemaphoreType.DMA((2, TILES)),
         ],
         compiler_params=pltpu.CompilerParams(
-            collective_id=0, has_side_effects=True, vmem_limit_bytes=40 * 1024 * 1024
+            collective_id=0, has_side_effects=True, vmem_limit_bytes=60 * 1024 * 1024
         ),
         cost_estimate=pl.CostEstimate(flops=800_000_000, bytes_accessed=2_000_000, transcendentals=0),
         name="shear_triples",
-    )(shear, weight, partner_tiles, pair_count, pair_bin, pair_angle)
+    )(shear, weight, partner_tiles, pair_count.reshape(1, 1), pair_bin, pair_angle)
     return flat.reshape(1, 1, 2 * LEGS * LEGS)
 
 

time: 53.4 us -> 49.9 us (0.934)
  local copies, waits for them, and re-layouts: 3.18 us -> 0.72 us
  Pallas kernels: 49.4 us -> 48.4 us
    unnamed x11 -> x1, local copies, waits for them, and re-layouts: 3.18 us -> 0.72 us
    pallas_call x1, Pallas kernels: 49.4 us -> 48.4 us  [per_device(): pl.pallas_call(kernel, out_shape=pltpu.VMEM((2 * LEGS * LEGS // LANES, LA...]
where the time goes in v2:
time: 49.9 us; the launch traced here: 49.8 us
  Pallas kernels  48.4 us (97%)
  local copies, waits for them, and re-layouts  0.72 us (1%)
  between operations  0.66 us (1%)
    pallas_call x1, Pallas kernels, per_device(): pl.pallas_call(kernel, out_shape=pltpu.VMEM((2 * LEGS * LEGS // LANES, LA...  48.4 us

profile of v2, /device:TPU:1, one launch (start us, length us, event | category | flops | bytes accessed | tf_op | source)
XLA Modules:
  0.0 49.8 jit_solution(3651099329512820793)
XLA Ops:
  0.7 48.4 %shear_triples.1 = f32[576,128]{1,0:T(8,128)S(1)} custom-call(f32[1,2,32]{2,1,0:T(2,128)} %shear_in.1, f32[1,32]{1,0:T(1,128)} %weight_in.1, s32[1,4]{1,0:T(1,128)} %partners_in.1, s32[1,1]{1,0:T(1,128)} %bitcast.2.count_in, s32[1,256,128]{2,1,0:T(8,128)} %bins_in.1, f32[1,256,128]{2,1,0:T(8,128)} %angles_in.1), custom_call_target="tpu_custom_call" | custom-call | flops 800000000 | bytes 2000000 | tf_op jit(solution)/shard_map/shear_triples/pallas_call | solution.py:310
  49.1 0.7 %copy.8 = f32[1,1,73728]{2,1,0:T(1,128)} copy(f32[1,1,73728]{2,1,0:T(1,128)S(1)} %bitcast.3) | data formatting | bytes 589824

commit v3 on v2

--- a/solution.py
+++ b/solution.py
@@ -204,13 +204,19 @@
                 [jnp.concatenate([hits[0], blank], axis=1), jnp.concatenate([blank, hits[1]], axis=1)],
                 axis=0,
             ).astype(jnp.bfloat16)
-            parts.append(
-                lax.dot_general(
-                    jnp.concatenate(terms, axis=1), onehot, (((1,), (1,)), ((), ())),
-                    preferred_element_type=jnp.float32,
-                )
-            )
-        table = jnp.concatenate(parts, axis=1)
+            parts.append((jnp.concatenate(terms, axis=1), onehot))
+        empty = jnp.zeros((2 * NR, 2 * LANES), jnp.bfloat16)
+        spread = jnp.concatenate(
+            [
+                jnp.concatenate([hit if a == b else empty for b, (_, hit) in enumerate(parts)], axis=1)
+                for a in range(ZB // 2)
+            ],
+            axis=0,
+        )
+        table = lax.dot_general(
+            jnp.concatenate([part for part, _ in parts], axis=1), spread, (((1,), (1,)), ((), ())),
+            preferred_element_type=jnp.float32,
+        )
         rows = pl.ds(local, NM, stride=HALF)
         grid0[rows, :] = table[:NM, :LANES]
         grid1[rows, :] = jnp.concatenate([table[:NM, LANES:], table[NM:, LANES:]], axis=1)
@@ -225,7 +231,7 @@
         )
 
     for half in range(2):
-        @pl.loop(0, HALF, unroll=2)
+        @pl.loop(0, HALF, unroll=HALF)
         def _(local):
             centre_table(half * HALF + local, local)
 

time: 49.9 us -> 47.9 us (0.960)
  Pallas kernels: 48.4 us -> 46.4 us
    pallas_call x1, Pallas kernels: 48.4 us -> 46.4 us  [per_device(): pl.pallas_call(kernel, out_shape=pltpu.VMEM((2 * LEGS * LEGS // LANES, LA...]
where the time goes in v3:
time: 47.9 us; the launch traced here: 47.8 us
  Pallas kernels  46.4 us (97%)
  local copies, waits for them, and re-layouts  0.72 us (2%)
  between operations  0.66 us (1%)
    pallas_call x1, Pallas kernels, per_device(): pl.pallas_call(kernel, out_shape=pltpu.VMEM((2 * LEGS * LEGS // LANES, LA...  46.4 us

profile of v3, /device:TPU:1, one launch (start us, length us, event | category | flops | bytes accessed | tf_op | source)
XLA Modules:
  0.0 47.8 jit_solution(9195973625066497380)
XLA Ops:
  0.7 46.4 %shear_triples.1 = f32[576,128]{1,0:T(8,128)S(1)} custom-call(f32[1,2,32]{2,1,0:T(2,128)} %shear_in.1, f32[1,32]{1,0:T(1,128)} %weight_in.1, s32[1,4]{1,0:T(1,128)} %partners_in.1, s32[1,1]{1,0:T(1,128)} %bitcast.2.count_in, s32[1,256,128]{2,1,0:T(8,128)} %bins_in.1, f32[1,256,128]{2,1,0:T(8,128)} %angles_in.1), custom_call_target="tpu_custom_call" | custom-call | flops 800000000 | bytes 2000000 | tf_op jit(solution)/shard_map/shear_triples/pallas_call | solution.py:316
  47.1 0.7 %copy.8 = f32[1,1,73728]{2,1,0:T(1,128)} copy(f32[1,1,73728]{2,1,0:T(1,128)S(1)} %bitcast.3) | data formatting | bytes 589824

commit v4 on v0

v4 whole, which is shorter than its diff:
```python
import jax
import jax.numpy as jnp
from jax import lax
from jax.experimental import pallas as pl
from jax.experimental.pallas import tpu as pltpu
from jax.sharding import PartitionSpec as P

GAL = 32
NM = 32
NR = 24
ZB = 8
TILES = 32
YS = 4
ZS = TILES // YS
FAR = ZS // 2
LANES = 128
HALF = 16
LEGS = ZB * NR
WIDE = 2 * LEGS
WINDOW = 4
PART = WINDOW * YS
TERMS = 2 * PART
MESH = pl.DeviceIdType.MESH


def sine_cosine(phi):
    half = phi * 0.5
    sq = half * half
    sin_h = -2.5052108385e-08
    for coefficient in (2.7557319224e-06, -1.9841269841e-04, 8.3333333333e-03, -1.6666666667e-01):
        sin_h = sin_h * sq + coefficient
    sin_h = half + half * (sq * sin_h)
    cos_h = 2.0876756988e-09
    for coefficient in (-2.7557319224e-07, 2.4801587302e-05, -1.3888888889e-03, 4.1666666667e-02, -0.5):
        cos_h = cos_h * sq + coefficient
    cos_h = 1.0 + sq * cos_h
    return 2.0 * sin_h * cos_h, 1.0 - 2.0 * sin_h * sin_h


def doubled(sine, cosine):
    return 2.0 * sine * cosine, 1.0 - 2.0 * sine * sine


def kernel(
    shear_in, weight_in, partners_in, count_in, bins_in, angles_in, out,
    shear, weight, partners, count, bins_all, bins_out, every, near, phi, bins_got, bins, sines, turns_c, turns_s,
    start, grid0, grid1, grid2, send, got, wide_re, wide_im, block_a, block_b,
    small_sem, own_sem, every_send, every_recv, raw_send, raw_recv, near_send, near_recv, tab_send, tab_recv,
):
    me_t = lax.axis_index("tile")
    me_z = lax.axis_index("zbin")
    at_z, at_y = me_t // YS, me_t % YS

    def tile_at(slot):
        return ((at_z + slot // YS) % ZS) * YS + (at_y + slot % YS) % YS

    def tile_from(slot):
        return ((at_z + ZS - slot // YS) % ZS) * YS + (at_y + YS - slot % YS) % YS

    def far_first(k):
        step = k // YS
        return (ZS // 2 + (step + 1) // 2 * (1 - 2 * (step % 2))) % ZS * YS + (k + 1) % YS

    def bin_at(step):
        return (me_z + step) % ZB

    def rows_of(centre_bin):
        return pl.ds(pl.multiple_of(centre_bin * GAL, GAL), GAL)

    opposite = ((at_z + FAR) % ZS) * YS + at_y

    small = [
        pltpu.make_async_copy(shear_in, shear, small_sem.at[0]),
        pltpu.make_async_copy(weight_in, weight, small_sem.at[1]),
        pltpu.make_async_copy(partners_in, partners, small_sem.at[2]),
        pltpu.make_async_copy(count_in, count, small_sem.at[3]),
    ]
    own_bins = pltpu.make_async_copy(bins_in.at[0], bins_all, own_sem.at[0])
    own_angles = pltpu.make_async_copy(angles_in.at[0, rows_of(me_z)], phi.at[0, me_z], own_sem.at[1])
    for copy in small:
        copy.start()
    own_bins.start()
    own_angles.start()
    barrier = pltpu.get_barrier_semaphore()

    @pl.loop(0, TILES - 1)
    def _(k):
        pl.semaphore_signal(barrier, inc=1, device_id={"tile": tile_at(far_first(k))}, device_id_type=MESH)

    @pl.loop(1, ZB)
    def _(step):
        pl.semaphore_signal(barrier, inc=1, device_id={"tile": opposite, "zbin": bin_at(step)}, device_id_type=MESH)

    @pl.loop(1, ZB)
    def _(step):
        pl.semaphore_signal(barrier, inc=1, device_id={"zbin": bin_at(step)}, device_id_type=MESH)

    for copy in small:
        copy.wait()
    lane = lax.broadcasted_iota(jnp.int32, (1, LANES), 1)
    place = lane // GAL
    wanted = jnp.full((1, LANES), partners[0, 0])
    for slot in range(1, LANES // GAL):
        wanted = jnp.where(place == slot, partners[0, slot], wanted)
    wanted = jnp.where(place < count[0, 0], wanted, -1).astype(jnp.float32)
    scaled = shear[0] * weight[...]
    every[0, 0:2, :] = jnp.concatenate([scaled] * (LANES // GAL), axis=1)
    every[0, 2:3, :] = wanted
    every[0, 3:4, :] = wanted
    own_bins.wait()

    @pl.loop(0, ZB)
    def _(c):
        bins_out[c] = bins_all[rows_of(c), :].astype(jnp.float32).astype(jnp.bfloat16)

    bins_got[0, me_z] = bins_out[me_z]
    pl.semaphore_wait(barrier, TILES - 1 + 2 * (ZB - 1))

    def every_copy(slot):
        return pltpu.make_async_remote_copy(
            src_ref=every.at[0], dst_ref=every.at[slot],
            send_sem=every_send.at[slot], recv_sem=every_recv.at[slot],
            device_id={"tile": tile_at(slot)}, device_id_type=MESH,
        )

    def raw_copies(side, step):
        to = bin_at(step)
        device = {"zbin": to} if side == 0 else {"tile": opposite, "zbin": to}
        pairs = ((angles_in.at[0, rows_of(to)], phi), (bins_out.at[to], bins_got))
        return [
            pltpu.make_async_remote_copy(
                src_ref=source, dst_ref=target.at[side, me_z],
                send_sem=raw_send.at[side, kind, step], recv_sem=raw_recv.at[side, kind, step],
                device_id=device, device_id_type=MESH,
            )
            for kind, (source, target) in enumerate(pairs)
        ]

    def near_copy(step):
        return pltpu.make_async_remote_copy(
            src_ref=near.at[me_z], dst_ref=near.at[me_z],
            send_sem=near_send.at[step], recv_sem=near_recv.at[step],
            device_id={"zbin": bin_at(step)}, device_id_type=MESH,
        )

    @pl.loop(0, TILES - 1)
    def _(k):
        every_copy(far_first(k)).start()

    @pl.loop(1, ZB)
    def _(step):
        for copy in raw_copies(0, step):
            copy.start()

    @pl.loop(0, ZB)
    def _(step):
        for copy in raw_copies(1, step):
            copy.start()

    own_angles.wait()

    @pl.loop(1, TILES)
    def _(slot):
        every_copy(slot).wait_recv()

    picked = [jnp.zeros((2, LANES), jnp.float32) for _ in range(2)]
    asked = [jnp.broadcast_to(every[slot, 2:3, :], (2, LANES)) for slot in (0, FAR * YS)]
    for slot in range(TILES):
        number = tile_from(slot).astype(jnp.float32)
        values = every[slot, 0:2, :]
        for side in range(2):
            picked[side] = picked[side] + jnp.where(asked[side] == number, values, 0.0)
    near[me_z] = jnp.concatenate(picked, axis=0)

    @pl.loop(1, ZB)
    def _(step):
        near_copy(step).start()

    def turns(side):
        @pl.loop(0, ZB)
        def _(z):
            sine, cosine = sine_cosine(phi[side, z])
            phi[side, z] = cosine
            sines[side, z] = sine
            bins[side, z] = bins_got[side, z].astype(jnp.float32)
            two = doubled(sine, cosine)
            four = doubled(*two)
            eight = doubled(*four)
            sixteen = doubled(*eight)
            for half in range(2):
                rows = slice(half * HALF, (half + 1) * HALF)
                group = (at_z + ZS - 1 - half) % ZS
                turn_s, turn_c = jnp.zeros((HALF, LANES)), jnp.ones((HALF, LANES))
                for bit, (step_s, step_c) in ((1, four), (2, eight), (4, sixteen)):
                    on = (group // bit) % 2 == 1
                    step_s = jnp.where(on, step_s[rows], 0.0)
                    step_c = jnp.where(on, step_c[rows], 1.0)
                    turn_s, turn_c = turn_s * step_c + turn_c * step_s, turn_c * step_c - turn_s * step_s
                for k in range(WINDOW):
                    turns_c[side, z, k, rows, :] = turn_c
                    turns_s[side, z, k, rows, :] = turn_s
                    wraps = (group + k + 1) % ZS == 0
                    step_s, step_c = four[0][rows], four[1][rows]
                    turn_s, turn_c = (
                        jnp.where(wraps, 0.0, turn_s * step_c + turn_c * step_s),
                        jnp.where(wraps, 1.0, turn_c * step_c - turn_s * step_s),
                    )

    def starts(side):
        @pl.loop(0, ZB)
        def _(z):
            cosine, sine = phi[side, z], sines[side, z]
            first = jnp.broadcast_to(near[z, 2 * side:2 * side + 1, :], (GAL, LANES))
            second = jnp.broadcast_to(near[z, 2 * side + 1:2 * side + 2, :], (GAL, LANES))
            twice = 2.0 * cosine
            base = pl.multiple_of(z * TERMS * GAL, TERMS * GAL)
            for k in range(WINDOW):
                turn_c, turn_s = turns_c[side, z, k], turns_s[side, z, k]
                old_re = first * turn_c + second * turn_s
                old_im = second * turn_c - first * turn_s
                new_re = old_re * cosine + old_im * sine
                new_im = old_im * cosine - old_re * sine
                for r in range(YS):
                    at = base + (k * YS + r) * GAL
                    start[side, pl.ds(at, GAL), :] = old_re
                    start[side, pl.ds(at + PART * GAL, GAL), :] = old_im
                    old_re, new_re = new_re, twice * new_re - old_re
                    old_im, new_im = new_im, twice * new_im - old_im

    level = lax.broadcasted_iota(jnp.int32, (NR, LANES), 0).astype(jnp.float32)
    blank = jnp.zeros((NR, LANES), jnp.float32)
    empty = jnp.zeros((2 * NR, 2 * LANES), jnp.bfloat16)

    def centre_table(side, i, local):
        terms, spread = [], []
        for pair in range(ZB // 2):
            hits = []
            for z in (2 * pair, 2 * pair + 1):
                rows = pl.ds(z * TERMS * GAL + i, TERMS, stride=GAL)
                terms.append(start[side, rows, :].astype(jnp.bfloat16))
                row = jnp.broadcast_to(bins[side, z, pl.ds(i, 1), :], (NR, LANES))
                hits.append(jnp.where(row == level, 1.0, 0.0))
            onehot = jnp.concatenate(
                [jnp.concatenate([hits[0], blank], axis=1), jnp.concatenate([blank, hits[1]], axis=1)],
                axis=0,
            ).astype(jnp.bfloat16)
            spread.append(
                jnp.concatenate([onehot if other == pair else empty for other in range(ZB // 2)], axis=1)
            )
        table = lax.dot_general(
            jnp.concatenate(terms, axis=1), jnp.concatenate(spread, axis=0), (((1,), (1,)), ((), ())),
            preferred_element_type=jnp.float32,
        )
        rows = pl.ds(local, PART, stride=HALF)
        grid0[rows, :] = table[:PART, :LANES]
        grid1[rows, :] = jnp.concatenate([table[:PART, LANES:], table[PART:, LANES:]], axis=1)
        grid2[rows, :] = table[PART:, :LANES]

    def block_rows(side, half, k, y):
        return ((side * WINDOW + k) * YS + y) * GAL + half * HALF

    def is_own(half, k, y):
        return k == 1 + half and y == 0

    def table_copy(side, half, k, y):
        chunk = 2 * side + half
        to_y = (at_y + y) % YS
        return pltpu.make_async_remote_copy(
            src_ref=send.at[chunk, k * YS + to_y],
            dst_ref=got.at[pl.ds(block_rows(side, half, k, y), HALF), :],
            send_sem=tab_send.at[chunk, k * YS + y], recv_sem=tab_recv.at[chunk, k * YS + y],
            device_id={"tile": ((at_z + ZS + k - 1 - half) % ZS) * YS + to_y}, device_id_type=MESH,
        )

    def tables(side):
        for half in range(2):
            chunk = 2 * side + half

            @pl.loop(0, HALF, unroll=HALF)
            def _(local):
                centre_table(side, half * HALF + local, local)

            @pl.loop(0, PART, unroll=4)
            def _(n):
                rows = pl.ds(pl.multiple_of(n * HALF, HALF), HALF)
                send[chunk, n, :, 0:LANES] = grid0[rows, :].astype(jnp.bfloat16)
                send[chunk, n, :, LANES:2 * LANES] = grid1[rows, :].astype(jnp.bfloat16)
                send[chunk, n, :, 2 * LANES:] = grid2[rows, :].astype(jnp.bfloat16)

            for k in ((3, 0, 2, 1), (0, 3, 1, 2))[half]:
                for y in (2, 1, 3, 0):
                    if is_own(half, k, y):
                        at = block_rows(side, half, k, y)
                        got[at:at + HALF, :] = send[chunk, k * YS + at_y]
                    else:
                        table_copy(side, half, k, y).start()

    @pl.loop(1, ZB)
    def _(step):
        for copy in raw_copies(0, step):
            copy.wait_recv()

    turns(0)

    @pl.loop(1, ZB)
    def _(step):
        near_copy(step).wait_recv()

    starts(0)
    tables(0)

    @pl.loop(0, ZB)
    def _(step):
        for copy in raw_copies(1, step):
            copy.wait_recv()

    turns(1)
    starts(1)
    tables(1)

    wide_re[...] = jnp.zeros_like(wide_re)
    wide_im[...] = jnp.zeros_like(wide_im)
    lane = lax.broadcasted_iota(jnp.int32, (2, LANES), 1)
    span = 2
    for side in range(2):
        for begin in range(0, WINDOW, span):
            scales = []
            for k in range(begin, begin + span):
                row = None
                for y in range(YS):
                    for half in range(2):
                        if not is_own(half, k, y):
                            table_copy(side, half, k, y).wait_recv()
                        source = (k - 1 - half - FAR * side) % ZS * YS + y
                        values = every[source, 0:2, :]
                        row = values if row is None else jnp.where(lane // HALF == 2 * y + half, values, row)
                scales.append(row)
            scales = jnp.concatenate(scales, axis=1)
            at = block_rows(side, 0, begin, 0)
            block = got[at:at + span * LANES, :]
            turned = block.T.astype(jnp.float32)
            first, second = scales[0:1], scales[1:2]
            real_in = turned[:LEGS]
            imag_in = jnp.concatenate([turned[WIDE - LANES:], turned[LEGS:WIDE - LANES]], axis=0)
            upper_re = (first * real_in - second * imag_in).astype(jnp.bfloat16)
            upper_im = (first * imag_in + second * real_in).astype(jnp.bfloat16)
            wide_re[...] += jnp.dot(upper_re, block, preferred_element_type=jnp.float32)
            wide_im[...] += jnp.dot(upper_im, block, preferred_element_type=jnp.float32)

    scale = float(TILES * GAL) ** -0.5
    low = lax.broadcasted_iota(jnp.int32, (LEGS // 2, LANES), 1) < LANES // 2
    for part in range(2):
        if part == 0:
            whole = wide_re[:, :LANES] + wide_im[:, 2 * LANES:]
            rest = wide_re[:, LANES:2 * LANES] + pltpu.roll(wide_im[:, LANES:2 * LANES], LANES // 2, 1)
        else:
            whole = wide_im[:, :LANES] - wide_re[:, 2 * LANES:]
            rest = wide_im[:, LANES:2 * LANES] - pltpu.roll(wide_re[:, LANES:2 * LANES], LANES // 2, 1)
        block_a[...] = whole * scale
        block_b[...] = rest * scale
        base = part * LEGS * LEGS // LANES
        even_a = block_a[pl.ds(0, LEGS // 2, stride=2), :]
        odd_a = pltpu.roll(block_a[pl.ds(1, LEGS // 2, stride=2), :], LANES // 2, 1)
        even_b = block_b[pl.ds(0, LEGS // 2, stride=2), :]
        odd_b = pltpu.roll(block_b[pl.ds(1, LEGS // 2, stride=2), :], LANES // 2, 1)
        out[pl.ds(base, LEGS // 2, stride=3), :] = even_a
        out[pl.ds(base + 1, LEGS // 2, stride=3), :] = jnp.where(low, even_b, odd_a)
        out[pl.ds(base + 2, LEGS // 2, stride=3), :] = jnp.where(low, odd_a, odd_b)

    for side in range(2):
        for half in range(2):
            for k in range(WINDOW):
                for y in range(YS):
                    if not is_own(half, k, y):
                        table_copy(side, half, k, y).wait_send()

    @pl.loop(1, TILES)
    def _(slot):
        every_copy(slot).wait_send()

    @pl.loop(1, ZB)
    def _(step):
        for copy in raw_copies(0, step):
            copy.wait_send()
        near_copy(step).wait_send()

    @pl.loop(0, ZB)
    def _(step):
        for copy in raw_copies(1, step):
            copy.wait_send()


def per_device(shear, weight, partner_tiles, pair_count, pair_bin, pair_angle):
    f32, bf16 = jnp.float32, jnp.bfloat16
    vmem, dma = pltpu.VMEM, pltpu.SemaphoreType.DMA
    flat = pl.pallas_call(
        kernel,
        out_shape=vmem((2 * LEGS * LEGS // LANES, LANES), f32),
        in_specs=[pl.BlockSpec(memory_space=pl.ANY)] * 6,
        out_specs=pl.BlockSpec(memory_space=vmem),
        scratch_shapes=[
            vmem((1, 2, GAL), f32),
            vmem((1, GAL), f32),
            pltpu.SMEM((1, LANES // GAL), jnp.int32),
            pltpu.SMEM((1, 1), jnp.int32),
            vmem((ZB * GAL, LANES), jnp.int32),
            vmem((ZB, GAL, LANES), bf16),
            vmem((TILES, 4, LANES), f32),
            vmem((ZB, 4, LANES), f32),
            vmem((2, ZB, GAL, LANES), f32),
            vmem((2, ZB, GAL, LANES), bf16),
            vmem((2, ZB, GAL, LANES), f32),
            vmem((2, ZB, GAL, LANES), f32),
            vmem((2, ZB, WINDOW, GAL, LANES), f32),
            vmem((2, ZB, WINDOW, GAL, LANES), f32),
            vmem((2, ZB * TERMS * GAL, LANES), f32),
            vmem((PART * HALF, LANES), f32),
            vmem((PART * HALF, LANES), f32),
            vmem((PART * HALF, LANES), f32),
            vmem((4, PART, HALF, WIDE), bf16),
            vmem((TILES * GAL, WIDE), bf16),
            vmem((LEGS, WIDE), f32),
            vmem((LEGS, WIDE), f32),
            vmem((LEGS, LANES), f32),
            vmem((LEGS, LANES), f32),
            dma((4,)),
            dma((2,)),
            dma((TILES,)),
            dma((TILES,)),
            dma((2, 2, ZB)),
            dma((2, 2, ZB)),
            dma((ZB,)),
            dma((ZB,)),
            dma((4, PART)),
            dma((4, PART)),
        ],
        compiler_params=pltpu.CompilerParams(
            collective_id=0, has_side_effects=True, vmem_limit_bytes=60 * 1024 * 1024
        ),
        cost_estimate=pl.CostEstimate(flops=800_000_000, bytes_accessed=2_000_000, transcendentals=0),
        name="shear_triples",
    )(shear, weight, partner_tiles, pair_count.reshape(1, 1), pair_bin, pair_angle)
    return flat.reshape(1, 1, 2 * LEGS * LEGS)


def solution(mesh):
    return jax.shard_map(
        per_device,
        mesh=mesh,
        in_specs=(
            P("zbin", None, "tile"),
            P("zbin", "tile"),
            P("tile", None),
            P("tile"),
            P("zbin", "tile", None),
            P("zbin", "tile", None),
        ),
        out_specs=P("zbin", "tile", None),
        check_vma=False,
    )
```

time: 632 us -> 45.7 us (0.07)
  waiting for transfers between devices: 232 us -> 0 us
  local copies, waits for them, and re-layouts: 178 us -> 0.72 us
  matrix products: 82.3 us -> 0 us
  other arithmetic: 62.1 us -> 0 us
  Pallas kernels: 0 us -> 44.2 us
  blocking collectives: 40.5 us -> 0 us
  starting transfers between devices: 17.4 us -> 0 us
  between operations: 16 us -> 0.66 us
    unnamed x2 -> x0, waiting for transfers between devices: 220 us -> none
    reshape x4 -> x0, local copies, waits for them, and re-layouts: 85 us -> none  [the longest x1 70.9 us: products(): jnp.stack([real_out, imag_out], axis=1).reshape(number, 2 * legs * legs)]
    dot_general x8 -> x0, matrix products: 82.3 us -> none  [the longest x4 29.4 us: slot_terms(): jnp.einsum('ijb,ijpn->ibpn', onehot, terms, preferred_element_type=jnp.fl...]
    another operation x5 -> x0, local copies, waits for them, and re-layouts: 67.2 us -> none  [the longest x1 41.3 us: products(): jnp.stack([real_out, imag_out], axis=1).reshape(number, 2 * legs * legs)]
    another operation x9 -> x0, other arithmetic: 54.8 us -> none  [the longest x1 37 us: products(): jnp.stack([real_out, imag_out], axis=1).reshape(number, 2 * legs * legs)]
    pallas_call x0 -> x1, Pallas kernels: none -> 44.2 us  [per_device(): pl.pallas_call(kernel, out_shape=vmem((2 * LEGS * LEGS // LANES, LANES),...]
    all_gather x1 -> x0, blocking collectives: 40.5 us -> none  [per_device(): everyone = lax.all_gather(packed, 'tile', axis=1, tiled=True)]
    all_to_all x1 -> x0, starting transfers between devices: 17.4 us -> none  [per_device(): lax.all_to_all(outgoing, 'zbin', split_axis=0, concat_axis=0, tiled=True)]
  transfers between devices with their start and end apart: 2 -> 0, of which waited for: 2 -> 0; matrix products, arithmetic and copies ran while one was open for 0% -> 0% of each run, Pallas kernels for 0% -> 0%
where the time goes in v4:
time: 45.7 us; the launch traced here: 45.6 us
  Pallas kernels  44.2 us (97%)
  local copies, waits for them, and re-layouts  0.72 us (2%)
  between operations  0.66 us (1%)
    pallas_call x1, Pallas kernels, per_device(): pl.pallas_call(kernel, out_shape=vmem((2 * LEGS * LEGS // LANES, LANES),...  44.2 us

profile of v4, /device:TPU:1, one launch (start us, length us, event | category | flops | bytes accessed | tf_op | source)
XLA Modules:
  0.0 45.6 jit_solution(10265910965933417275)
XLA Ops:
  0.7 44.2 %shear_triples.1 = f32[576,128]{1,0:T(8,128)S(1)} custom-call(f32[1,2,32]{2,1,0:T(2,128)} %shear_in.1, f32[1,32]{1,0:T(1,128)} %weight_in.1, s32[1,4]{1,0:T(1,128)} %partners_in.1, s32[1,1]{1,0:T(1,128)} %bitcast.2.count_in, s32[1,256,128]{2,1,0:T(8,128)} %bins_in.1, f32[1,256,128]{2,1,0:T(8,128)} %angles_in.1), custom_call_target="tpu_custom_call" | custom-call | flops 800000000 | bytes 2000000 | tf_op jit(solution)/shard_map/shear_triples/pallas_call | solution.py:396
  44.9 0.7 %copy.8 = f32[1,1,73728]{2,1,0:T(1,128)} copy(f32[1,1,73728]{2,1,0:T(1,128)S(1)} %bitcast.3) | data formatting | bytes 589824

commit v5 on v4

--- a/solution.py
+++ b/solution.py
@@ -20,6 +20,7 @@
 WINDOW = 4
 PART = WINDOW * YS
 TERMS = 2 * PART
+CODE = 10430.0
 MESH = pl.DeviceIdType.MESH
 
 
@@ -43,31 +44,32 @@
 
 def kernel(
     shear_in, weight_in, partners_in, count_in, bins_in, angles_in, out,
-    shear, weight, partners, count, bins_all, bins_out, every, near, phi, bins_got, bins, sines, turns_c, turns_s,
+    shear, weight, partners, count, bins_all, angles_all, coded, every, near, raw, bins, cosines, sines, turns_c, turns_s,
     start, grid0, grid1, grid2, send, got, wide_re, wide_im, block_a, block_b,
     small_sem, own_sem, every_send, every_recv, raw_send, raw_recv, near_send, near_recv, tab_send, tab_recv,
 ):
     me_t = lax.axis_index("tile")
     me_z = lax.axis_index("zbin")
     at_z, at_y = me_t // YS, me_t % YS
+    z_at = [at_z * YS] + [(at_z + step) % ZS * YS for step in range(1, ZS)]
+    y_at = [at_y] + [(at_y + step) % YS for step in range(1, YS)]
+    bin_at = [me_z] + [(me_z + step) % ZB for step in range(1, ZB)]
+    opposite = z_at[FAR] + at_y
 
     def tile_at(slot):
-        return ((at_z + slot // YS) % ZS) * YS + (at_y + slot % YS) % YS
+        return z_at[slot // YS] + y_at[slot % YS]
 
     def tile_from(slot):
-        return ((at_z + ZS - slot // YS) % ZS) * YS + (at_y + YS - slot % YS) % YS
-
-    def far_first(k):
-        step = k // YS
-        return (ZS // 2 + (step + 1) // 2 * (1 - 2 * (step % 2))) % ZS * YS + (k + 1) % YS
-
-    def bin_at(step):
-        return (me_z + step) % ZB
+        return z_at[-(slot // YS) % ZS] + y_at[-(slot % YS) % YS]
+
+    def hops(slot):
+        return min(slot // YS, ZS - slot // YS) + min(slot % YS, YS - slot % YS)
+
+    far_first = sorted(range(1, TILES), key=lambda slot: -hops(slot))
+    steps_far_first = (4, 3, 5, 2, 6, 7, 1)
 
     def rows_of(centre_bin):
         return pl.ds(pl.multiple_of(centre_bin * GAL, GAL), GAL)
-
-    opposite = ((at_z + FAR) % ZS) * YS + at_y
 
     small = [
         pltpu.make_async_copy(shear_in, shear, small_sem.at[0]),
@@ -75,25 +77,23 @@
         pltpu.make_async_copy(partners_in, partners, small_sem.at[2]),
         pltpu.make_async_copy(count_in, count, small_sem.at[3]),
     ]
-    own_bins = pltpu.make_async_copy(bins_in.at[0], bins_all, own_sem.at[0])
-    own_angles = pltpu.make_async_copy(angles_in.at[0, rows_of(me_z)], phi.at[0, me_z], own_sem.at[1])
-    for copy in small:
+    own = [
+        pltpu.make_async_copy(bins_in.at[0], bins_all, own_sem.at[0]),
+        pltpu.make_async_copy(angles_in.at[0], angles_all, own_sem.at[1]),
+    ]
+    for copy in small + own:
         copy.start()
-    own_bins.start()
-    own_angles.start()
     barrier = pltpu.get_barrier_semaphore()
 
-    @pl.loop(0, TILES - 1)
-    def _(k):
-        pl.semaphore_signal(barrier, inc=1, device_id={"tile": tile_at(far_first(k))}, device_id_type=MESH)
-
-    @pl.loop(1, ZB)
-    def _(step):
-        pl.semaphore_signal(barrier, inc=1, device_id={"tile": opposite, "zbin": bin_at(step)}, device_id_type=MESH)
-
-    @pl.loop(1, ZB)
-    def _(step):
-        pl.semaphore_signal(barrier, inc=1, device_id={"zbin": bin_at(step)}, device_id_type=MESH)
+    def greet(tile, zbin):
+        pl.semaphore_signal(barrier, inc=1, device_id=(tile, zbin), device_id_type=MESH)
+
+    for step in steps_far_first:
+        greet(opposite, bin_at[step])
+    for slot in far_first:
+        greet(tile_at(slot), me_z)
+    for step in steps_far_first:
+        greet(me_t, bin_at[step])
 
     for copy in small:
         copy.wait()
@@ -107,60 +107,56 @@
     every[0, 0:2, :] = jnp.concatenate([scaled] * (LANES // GAL), axis=1)
     every[0, 2:3, :] = wanted
     every[0, 3:4, :] = wanted
-    own_bins.wait()
+    for copy in own:
+        copy.wait()
 
     @pl.loop(0, ZB)
     def _(c):
-        bins_out[c] = bins_all[rows_of(c), :].astype(jnp.float32).astype(jnp.bfloat16)
-
-    bins_got[0, me_z] = bins_out[me_z]
+        angles = angles_all[rows_of(c), :] * CODE
+        angles = (angles + jnp.where(angles < 0.0, -0.5, 0.5)).astype(jnp.int32).astype(jnp.int16)
+        numbers = bins_all[rows_of(c), :].astype(jnp.int16)
+        for half in range(2):
+            coded[c, half, 0] = angles[half * HALF:(half + 1) * HALF]
+            coded[c, half, 1] = numbers[half * HALF:(half + 1) * HALF]
+
+    raw[0, me_z] = coded[me_z]
     pl.semaphore_wait(barrier, TILES - 1 + 2 * (ZB - 1))
 
     def every_copy(slot):
         return pltpu.make_async_remote_copy(
             src_ref=every.at[0], dst_ref=every.at[slot],
             send_sem=every_send.at[slot], recv_sem=every_recv.at[slot],
-            device_id={"tile": tile_at(slot)}, device_id_type=MESH,
-        )
-
-    def raw_copies(side, step):
-        to = bin_at(step)
-        device = {"zbin": to} if side == 0 else {"tile": opposite, "zbin": to}
-        pairs = ((angles_in.at[0, rows_of(to)], phi), (bins_out.at[to], bins_got))
-        return [
-            pltpu.make_async_remote_copy(
-                src_ref=source, dst_ref=target.at[side, me_z],
-                send_sem=raw_send.at[side, kind, step], recv_sem=raw_recv.at[side, kind, step],
-                device_id=device, device_id_type=MESH,
-            )
-            for kind, (source, target) in enumerate(pairs)
-        ]
+            device_id=(tile_at(slot), me_z), device_id_type=MESH,
+        )
+
+    def raw_copy(step):
+        return pltpu.make_async_remote_copy(
+            src_ref=coded.at[bin_at[step]], dst_ref=raw.at[0, me_z],
+            send_sem=raw_send.at[0, step], recv_sem=raw_recv.at[0, step],
+            device_id=(me_t, bin_at[step]), device_id_type=MESH,
+        )
+
+    def far_copy(half, step):
+        return pltpu.make_async_remote_copy(
+            src_ref=coded.at[bin_at[step], half], dst_ref=raw.at[1, me_z, half],
+            send_sem=raw_send.at[1 + half, step], recv_sem=raw_recv.at[1 + half, step],
+            device_id=(opposite, bin_at[step]), device_id_type=MESH,
+        )
 
     def near_copy(step):
         return pltpu.make_async_remote_copy(
             src_ref=near.at[me_z], dst_ref=near.at[me_z],
             send_sem=near_send.at[step], recv_sem=near_recv.at[step],
-            device_id={"zbin": bin_at(step)}, device_id_type=MESH,
-        )
-
-    @pl.loop(0, TILES - 1)
-    def _(k):
-        every_copy(far_first(k)).start()
-
-    @pl.loop(1, ZB)
-    def _(step):
-        for copy in raw_copies(0, step):
-            copy.start()
-
-    @pl.loop(0, ZB)
-    def _(step):
-        for copy in raw_copies(1, step):
-            copy.start()
-
-    own_angles.wait()
-
-    @pl.loop(1, TILES)
-    def _(slot):
+            device_id=(me_t, bin_at[step]), device_id_type=MESH,
+        )
+
+    for slot in far_first:
+        every_copy(slot).start()
+    for step in steps_far_first:
+        raw_copy(step).start()
+    for step in steps_far_first + (0,):
+        far_copy(0, step).start()
+    for slot in far_first:
         every_copy(slot).wait_recv()
 
     picked = [jnp.zeros((2, LANES), jnp.float32) for _ in range(2)]
@@ -171,59 +167,61 @@
         for side in range(2):
             picked[side] = picked[side] + jnp.where(asked[side] == number, values, 0.0)
     near[me_z] = jnp.concatenate(picked, axis=0)
-
-    @pl.loop(1, ZB)
-    def _(step):
+    for step in steps_far_first:
         near_copy(step).start()
-
-    def turns(side):
+    for step in steps_far_first + (0,):
+        far_copy(1, step).start()
+
+    def turns(side, half):
+        rows = slice(half * HALF, (half + 1) * HALF)
+        group = (at_z + ZS - 1 - half) % ZS
+
         @pl.loop(0, ZB)
         def _(z):
-            sine, cosine = sine_cosine(phi[side, z])
-            phi[side, z] = cosine
-            sines[side, z] = sine
-            bins[side, z] = bins_got[side, z].astype(jnp.float32)
-            two = doubled(sine, cosine)
-            four = doubled(*two)
+            angles = raw[side, z, half, 0].astype(jnp.int32).astype(jnp.float32) * (1.0 / CODE)
+            bins[side, z, rows, :] = raw[side, z, half, 1].astype(jnp.int32).astype(jnp.float32)
+            sine, cosine = sine_cosine(angles)
+            cosines[side, z, rows, :] = cosine
+            sines[side, z, rows, :] = sine
+            four = doubled(*doubled(sine, cosine))
             eight = doubled(*four)
             sixteen = doubled(*eight)
-            for half in range(2):
-                rows = slice(half * HALF, (half + 1) * HALF)
-                group = (at_z + ZS - 1 - half) % ZS
-                turn_s, turn_c = jnp.zeros((HALF, LANES)), jnp.ones((HALF, LANES))
-                for bit, (step_s, step_c) in ((1, four), (2, eight), (4, sixteen)):
-                    on = (group // bit) % 2 == 1
-                    step_s = jnp.where(on, step_s[rows], 0.0)
-                    step_c = jnp.where(on, step_c[rows], 1.0)
-                    turn_s, turn_c = turn_s * step_c + turn_c * step_s, turn_c * step_c - turn_s * step_s
-                for k in range(WINDOW):
-                    turns_c[side, z, k, rows, :] = turn_c
-                    turns_s[side, z, k, rows, :] = turn_s
-                    wraps = (group + k + 1) % ZS == 0
-                    step_s, step_c = four[0][rows], four[1][rows]
-                    turn_s, turn_c = (
-                        jnp.where(wraps, 0.0, turn_s * step_c + turn_c * step_s),
-                        jnp.where(wraps, 1.0, turn_c * step_c - turn_s * step_s),
-                    )
-
-    def starts(side):
+            turn_s, turn_c = jnp.zeros((HALF, LANES)), jnp.ones((HALF, LANES))
+            for bit, (step_s, step_c) in ((1, four), (2, eight), (4, sixteen)):
+                on = (group // bit) % 2 == 1
+                step_s = jnp.where(on, step_s, 0.0)
+                step_c = jnp.where(on, step_c, 1.0)
+                turn_s, turn_c = turn_s * step_c + turn_c * step_s, turn_c * step_c - turn_s * step_s
+            for k in range(WINDOW):
+                turns_c[side, z, k, rows, :] = turn_c
+                turns_s[side, z, k, rows, :] = turn_s
+                wraps = (group + k + 1) % ZS == 0
+                step_s, step_c = four
+                turn_s, turn_c = (
+                    jnp.where(wraps, 0.0, turn_s * step_c + turn_c * step_s),
+                    jnp.where(wraps, 1.0, turn_c * step_c - turn_s * step_s),
+                )
+
+    def starts(side, half):
+        rows = slice(half * HALF, (half + 1) * HALF)
+
         @pl.loop(0, ZB)
         def _(z):
-            cosine, sine = phi[side, z], sines[side, z]
-            first = jnp.broadcast_to(near[z, 2 * side:2 * side + 1, :], (GAL, LANES))
-            second = jnp.broadcast_to(near[z, 2 * side + 1:2 * side + 2, :], (GAL, LANES))
+            cosine, sine = cosines[side, z, rows, :], sines[side, z, rows, :]
+            first = jnp.broadcast_to(near[z, 2 * side:2 * side + 1, :], (HALF, LANES))
+            second = jnp.broadcast_to(near[z, 2 * side + 1:2 * side + 2, :], (HALF, LANES))
             twice = 2.0 * cosine
-            base = pl.multiple_of(z * TERMS * GAL, TERMS * GAL)
+            base = pl.multiple_of(z * TERMS * GAL, TERMS * GAL) + half * HALF
             for k in range(WINDOW):
-                turn_c, turn_s = turns_c[side, z, k], turns_s[side, z, k]
+                turn_c, turn_s = turns_c[side, z, k, rows, :], turns_s[side, z, k, rows, :]
                 old_re = first * turn_c + second * turn_s
                 old_im = second * turn_c - first * turn_s
                 new_re = old_re * cosine + old_im * sine
                 new_im = old_im * cosine - old_re * sine
                 for r in range(YS):
                     at = base + (k * YS + r) * GAL
-                    start[side, pl.ds(at, GAL), :] = old_re
-                    start[side, pl.ds(at + PART * GAL, GAL), :] = old_im
+                    start[side, pl.ds(at, HALF), :] = old_re
+                    start[side, pl.ds(at + PART * GAL, HALF), :] = old_im
                     old_re, new_re = new_re, twice * new_re - old_re
                     old_im, new_im = new_im, twice * new_im - old_im
 
@@ -264,59 +262,51 @@
 
     def table_copy(side, half, k, y):
         chunk = 2 * side + half
-        to_y = (at_y + y) % YS
+        to_y = y_at[y]
         return pltpu.make_async_remote_copy(
             src_ref=send.at[chunk, k * YS + to_y],
             dst_ref=got.at[pl.ds(block_rows(side, half, k, y), HALF), :],
             send_sem=tab_send.at[chunk, k * YS + y], recv_sem=tab_recv.at[chunk, k * YS + y],
-            device_id={"tile": ((at_z + ZS + k - 1 - half) % ZS) * YS + to_y}, device_id_type=MESH,
-        )
-
-    def tables(side):
-        for half in range(2):
-            chunk = 2 * side + half
-
-            @pl.loop(0, HALF, unroll=HALF)
-            def _(local):
-                centre_table(side, half * HALF + local, local)
-
-            @pl.loop(0, PART, unroll=4)
-            def _(n):
-                rows = pl.ds(pl.multiple_of(n * HALF, HALF), HALF)
-                send[chunk, n, :, 0:LANES] = grid0[rows, :].astype(jnp.bfloat16)
-                send[chunk, n, :, LANES:2 * LANES] = grid1[rows, :].astype(jnp.bfloat16)
-                send[chunk, n, :, 2 * LANES:] = grid2[rows, :].astype(jnp.bfloat16)
-
-            for k in ((3, 0, 2, 1), (0, 3, 1, 2))[half]:
-                for y in (2, 1, 3, 0):
-                    if is_own(half, k, y):
-                        at = block_rows(side, half, k, y)
-                        got[at:at + HALF, :] = send[chunk, k * YS + at_y]
-                    else:
-                        table_copy(side, half, k, y).start()
-
-    @pl.loop(1, ZB)
-    def _(step):
-        for copy in raw_copies(0, step):
-            copy.wait_recv()
-
-    turns(0)
-
-    @pl.loop(1, ZB)
-    def _(step):
+            device_id=(z_at[(k - 1 - half) % ZS] + to_y, me_z), device_id_type=MESH,
+        )
+
+    def tables(side, half):
+        chunk = 2 * side + half
+
+        @pl.loop(0, HALF, unroll=HALF)
+        def _(local):
+            centre_table(side, half * HALF + local, local)
+
+        @pl.loop(0, PART, unroll=4)
+        def _(n):
+            rows = pl.ds(pl.multiple_of(n * HALF, HALF), HALF)
+            send[chunk, n, :, 0:LANES] = grid0[rows, :].astype(jnp.bfloat16)
+            send[chunk, n, :, LANES:2 * LANES] = grid1[rows, :].astype(jnp.bfloat16)
+            send[chunk, n, :, 2 * LANES:] = grid2[rows, :].astype(jnp.bfloat16)
+
+        for k in ((3, 0, 2, 1), (0, 3, 1, 2))[half]:
+            for y in (2, 1, 3, 0):
+                if is_own(half, k, y):
+                    at = block_rows(side, half, k, y)
+                    got[at:at + HALF, :] = send[chunk, k * YS + at_y]
+                else:
+                    table_copy(side, half, k, y).start()
+
+    for step in steps_far_first:
+        raw_copy(step).wait_recv()
+    turns(0, 0)
+    turns(0, 1)
+    for step in steps_far_first:
         near_copy(step).wait_recv()
-
-    starts(0)
-    tables(0)
-
-    @pl.loop(0, ZB)
-    def _(step):
-        for copy in raw_copies(1, step):
-            copy.wait_recv()
-
-    turns(1)
-    starts(1)
-    tables(1)
+    for half in range(2):
+        starts(0, half)
+        tables(0, half)
+    for half in range(2):
+        for step in steps_far_first + (0,):
+            far_copy(half, step).wait_recv()
+        turns(1, half)
+        starts(1, half)
+        tables(1, half)
 
     wide_re[...] = jnp.zeros_like(wide_re)
     wide_im[...] = jnp.zeros_like(wide_im)
@@ -374,20 +364,14 @@
                     if not is_own(half, k, y):
                         table_copy(side, half, k, y).wait_send()
 
-    @pl.loop(1, TILES)
-    def _(slot):
+    for slot in far_first:
         every_copy(slot).wait_send()
-
-    @pl.loop(1, ZB)
-    def _(step):
-        for copy in raw_copies(0, step):
-            copy.wait_send()
+    for step in steps_far_first:
+        raw_copy(step).wait_send()
         near_copy(step).wait_send()
-
-    @pl.loop(0, ZB)
-    def _(step):
-        for copy in raw_copies(1, step):
-            copy.wait_send()
+    for step in steps_far_first + (0,):
+        for half in range(2):
+            far_copy(half, step).wait_send()
 
 
 def per_device(shear, weight, partner_tiles, pair_count, pair_bin, pair_angle):
@@ -404,11 +388,12 @@
             pltpu.SMEM((1, LANES // GAL), jnp.int32),
             pltpu.SMEM((1, 1), jnp.int32),
             vmem((ZB * GAL, LANES), jnp.int32),
-            vmem((ZB, GAL, LANES), bf16),
+            vmem((ZB * GAL, LANES), f32),
+            vmem((ZB, 2, 2, HALF, LANES), jnp.int16),
             vmem((TILES, 4, LANES), f32),
             vmem((ZB, 4, LANES), f32),
+            vmem((2, ZB, 2, 2, HALF, LANES), jnp.int16),
             vmem((2, ZB, GAL, LANES), f32),
-            vmem((2, ZB, GAL, LANES), bf16),
             vmem((2, ZB, GAL, LANES), f32),
             vmem((2, ZB, GAL, LANES), f32),
             vmem((2, ZB, WINDOW, GAL, LANES), f32),
@@ -427,8 +412,8 @@
             dma((2,)),
             dma((TILES,)),
             dma((TILES,)),
-            dma((2, 2, ZB)),
-            dma((2, 2, ZB)),
+            dma((3, ZB)),
+            dma((3, ZB)),
             dma((ZB,)),
             dma((ZB,)),
             dma((4, PART)),

time: 45.7 us -> 39.4 us (0.86)
  Pallas kernels: 44.2 us -> 37.9 us
    pallas_call x1, Pallas kernels: 44.2 us -> 37.9 us  [per_device(): pl.pallas_call(kernel, out_shape=vmem((2 * LEGS * LEGS // LANES, LANES),...]
where the time goes in v5:
time: 39.4 us; the launch traced here: 39.3 us
  Pallas kernels  37.9 us (96%)
  local copies, waits for them, and re-layouts  0.72 us (2%)
  between operations  0.66 us (2%)
    pallas_call x1, Pallas kernels, per_device(): pl.pallas_call(kernel, out_shape=vmem((2 * LEGS * LEGS // LANES, LANES),...  37.9 us

profile of v5, /device:TPU:1, one launch (start us, length us, event | category | flops | bytes accessed | tf_op | source)
XLA Modules:
  0.0 39.3 jit_solution(3753936141924133204)
XLA Ops:
  0.7 37.9 %shear_triples.1 = f32[576,128]{1,0:T(8,128)S(1)} custom-call(f32[1,2,32]{2,1,0:T(2,128)} %shear_in.1, f32[1,32]{1,0:T(1,128)} %weight_in.1, s32[1,4]{1,0:T(1,128)} %partners_in.1, s32[1,1]{1,0:T(1,128)} %bitcast.2.count_in, s32[1,256,128]{2,1,0:T(8,128)} %bins_in.1, f32[1,256,128]{2,1,0:T(8,128)} %angles_in.1), custom_call_target="tpu_custom_call" | custom-call | flops 800000000 | bytes 2000000 | tf_op jit(solution)/shard_map/shear_triples/pallas_call | solution.py:380
  38.6 0.7 %copy.8 = f32[1,1,73728]{2,1,0:T(1,128)} copy(f32[1,1,73728]{2,1,0:T(1,128)S(1)} %bitcast.3) | data formatting | bytes 589824

commit v6 on v5

--- a/solution.py
+++ b/solution.py
@@ -20,6 +20,8 @@
 WINDOW = 4
 PART = WINDOW * YS
 TERMS = 2 * PART
+PITCH = GAL + 4
+SPLIT = LANES - 4 * NR
 CODE = 10430.0
 MESH = pl.DeviceIdType.MESH
 
@@ -205,13 +207,13 @@
     def starts(side, half):
         rows = slice(half * HALF, (half + 1) * HALF)
 
-        @pl.loop(0, ZB)
+        @pl.loop(0, ZB, unroll=ZB)
         def _(z):
             cosine, sine = cosines[side, z, rows, :], sines[side, z, rows, :]
             first = jnp.broadcast_to(near[z, 2 * side:2 * side + 1, :], (HALF, LANES))
             second = jnp.broadcast_to(near[z, 2 * side + 1:2 * side + 2, :], (HALF, LANES))
             twice = 2.0 * cosine
-            base = pl.multiple_of(z * TERMS * GAL, TERMS * GAL) + half * HALF
+            base = z * TERMS * PITCH + half * HALF
             for k in range(WINDOW):
                 turn_c, turn_s = turns_c[side, z, k, rows, :], turns_s[side, z, k, rows, :]
                 old_re = first * turn_c + second * turn_s
@@ -219,40 +221,49 @@
                 new_re = old_re * cosine + old_im * sine
                 new_im = old_im * cosine - old_re * sine
                 for r in range(YS):
-                    at = base + (k * YS + r) * GAL
+                    at = base + (k * YS + r) * PITCH
                     start[side, pl.ds(at, HALF), :] = old_re
-                    start[side, pl.ds(at + PART * GAL, HALF), :] = old_im
+                    start[side, pl.ds(at + PART * PITCH, HALF), :] = old_im
                     old_re, new_re = new_re, twice * new_re - old_re
                     old_im, new_im = new_im, twice * new_im - old_im
 
     level = lax.broadcasted_iota(jnp.int32, (NR, LANES), 0).astype(jnp.float32)
-    blank = jnp.zeros((NR, LANES), jnp.float32)
-    empty = jnp.zeros((2 * NR, 2 * LANES), jnp.bfloat16)
+    lane = lax.broadcasted_iota(jnp.int32, (TERMS, LANES), 1)
+
+    def line(piece, place):
+        blank = jnp.zeros_like(piece)
+        return jnp.concatenate([piece if at == place else blank for at in range(ZB // 2)], axis=1)
+
+    def product(terms, lines):
+        onehots = jnp.concatenate(lines, axis=0).astype(jnp.bfloat16)
+        return lax.dot_general(
+            jnp.concatenate(terms, axis=1), onehots, (((1,), (1,)), ((), ())), preferred_element_type=jnp.float32
+        )
 
     def centre_table(side, i, local):
-        terms, spread = [], []
-        for pair in range(ZB // 2):
-            hits = []
-            for z in (2 * pair, 2 * pair + 1):
-                rows = pl.ds(z * TERMS * GAL + i, TERMS, stride=GAL)
-                terms.append(start[side, rows, :].astype(jnp.bfloat16))
-                row = jnp.broadcast_to(bins[side, z, pl.ds(i, 1), :], (NR, LANES))
-                hits.append(jnp.where(row == level, 1.0, 0.0))
-            onehot = jnp.concatenate(
-                [jnp.concatenate([hits[0], blank], axis=1), jnp.concatenate([blank, hits[1]], axis=1)],
-                axis=0,
-            ).astype(jnp.bfloat16)
-            spread.append(
-                jnp.concatenate([onehot if other == pair else empty for other in range(ZB // 2)], axis=1)
-            )
-        table = lax.dot_general(
-            jnp.concatenate(terms, axis=1), jnp.concatenate(spread, axis=0), (((1,), (1,)), ((), ())),
-            preferred_element_type=jnp.float32,
-        )
+        terms, hits = [], []
+        for z in range(ZB):
+            rows = pl.ds(z * TERMS * PITCH + i, TERMS, stride=PITCH)
+            terms.append(start[side, rows, :].astype(jnp.bfloat16))
+            row = jnp.broadcast_to(bins[side, z, pl.ds(i, 1), :], (NR, LANES))
+            hits.append(jnp.where(row == level, 1.0, 0.0))
+        cut = SPLIT - NR
+        table0 = product(terms[:4], [line(hits[z], z) for z in range(4)])
+        table1 = product(
+            terms[4:],
+            [
+                line(hits[5][cut:], 1), line(hits[6], 2), line(hits[7], 3),
+                jnp.zeros((SPLIT, 4 * LANES)), line(hits[4], 0), line(hits[5][:cut], 1),
+            ],
+        )
+        table0 = jnp.concatenate([table0, jnp.zeros((TERMS, SPLIT))], axis=1)
+        front = jnp.where(lane < LANES - SPLIT, table0, table1)
         rows = pl.ds(local, PART, stride=HALF)
-        grid0[rows, :] = table[:PART, :LANES]
-        grid1[rows, :] = jnp.concatenate([table[:PART, LANES:], table[PART:, LANES:]], axis=1)
-        grid2[rows, :] = table[PART:, :LANES]
+        grid0[rows, :] = front[:PART]
+        grid1[rows, :] = jnp.where(
+            lane[:PART] < LANES // 2, table1[:PART], pltpu.roll(table1[PART:], LANES // 2, 1)
+        )
+        grid2[rows, :] = front[PART:]
 
     def block_rows(side, half, k, y):
         return ((side * WINDOW + k) * YS + y) * GAL + half * HALF
@@ -277,7 +288,7 @@
         def _(local):
             centre_table(side, half * HALF + local, local)
 
-        @pl.loop(0, PART, unroll=4)
+        @pl.loop(0, PART, unroll=PART)
         def _(n):
             rows = pl.ds(pl.multiple_of(n * HALF, HALF), HALF)
             send[chunk, n, :, 0:LANES] = grid0[rows, :].astype(jnp.bfloat16)
@@ -398,7 +409,7 @@
             vmem((2, ZB, GAL, LANES), f32),
             vmem((2, ZB, WINDOW, GAL, LANES), f32),
             vmem((2, ZB, WINDOW, GAL, LANES), f32),
-            vmem((2, ZB * TERMS * GAL, LANES), f32),
+            vmem((2, ZB * TERMS * PITCH, LANES), f32),
             vmem((PART * HALF, LANES), f32),
             vmem((PART * HALF, LANES), f32),
             vmem((PART * HALF, LANES), f32),

time: 39.4 us -> 38.3 us (0.972)
  Pallas kernels: 37.9 us -> 36.9 us
    pallas_call x1, Pallas kernels: 37.9 us -> 36.9 us  [per_device(): pl.pallas_call(kernel, out_shape=vmem((2 * LEGS * LEGS // LANES, LANES),...]
where the time goes in v6:
time: 38.3 us; the launch traced here: 38.2 us
  Pallas kernels  36.9 us (96%)
  local copies, waits for them, and re-layouts  0.72 us (2%)
  between operations  0.66 us (2%)
    pallas_call x1, Pallas kernels, per_device(): pl.pallas_call(kernel, out_shape=vmem((2 * LEGS * LEGS // LANES, LANES),...  36.9 us

profile of v6, /device:TPU:1, one launch (start us, length us, event | category | flops | bytes accessed | tf_op | source)
XLA Modules:
  0.0 38.2 jit_solution(945317163456278534)
XLA Ops:
  0.7 36.9 %shear_triples.1 = f32[576,128]{1,0:T(8,128)S(1)} custom-call(f32[1,2,32]{2,1,0:T(2,128)} %shear_in.1, f32[1,32]{1,0:T(1,128)} %weight_in.1, s32[1,4]{1,0:T(1,128)} %partners_in.1, s32[1,1]{1,0:T(1,128)} %bitcast.2.count_in, s32[1,256,128]{2,1,0:T(8,128)} %bins_in.1, f32[1,256,128]{2,1,0:T(8,128)} %angles_in.1), custom_call_target="tpu_custom_call" | custom-call | flops 800000000 | bytes 2000000 | tf_op jit(solution)/shard_map/shear_triples/pallas_call | solution.py:391
  37.5 0.7 %copy.8 = f32[1,1,73728]{2,1,0:T(1,128)} copy(f32[1,1,73728]{2,1,0:T(1,128)S(1)} %bitcast.3) | data formatting | bytes 589824

commit v7 on v6

--- a/solution.py
+++ b/solution.py
@@ -319,12 +319,32 @@
         starts(1, half)
         tables(1, half)
 
+    def sent(chunks):
+        for side, half in chunks:
+            for k in range(WINDOW):
+                for y in range(YS):
+                    if not is_own(half, k, y):
+                        table_copy(side, half, k, y).wait_send()
+
+    for slot in far_first:
+        every_copy(slot).wait_send()
+    for step in steps_far_first:
+        raw_copy(step).wait_send()
+        near_copy(step).wait_send()
+    for step in steps_far_first + (0,):
+        for half in range(2):
+            far_copy(half, step).wait_send()
+
     wide_re[...] = jnp.zeros_like(wide_re)
     wide_im[...] = jnp.zeros_like(wide_im)
     lane = lax.broadcasted_iota(jnp.int32, (2, LANES), 1)
     span = 2
     for side in range(2):
         for begin in range(0, WINDOW, span):
+            if (side, begin) == (1, 0):
+                sent([(0, 0), (0, 1)])
+            if (side, begin) == (1, span):
+                sent([(1, 0), (1, 1)])
             scales = []
             for k in range(begin, begin + span):
                 row = None
@@ -367,22 +387,6 @@
         out[pl.ds(base, LEGS // 2, stride=3), :] = even_a
         out[pl.ds(base + 1, LEGS // 2, stride=3), :] = jnp.where(low, even_b, odd_a)
         out[pl.ds(base + 2, LEGS // 2, stride=3), :] = jnp.where(low, odd_a, odd_b)
-
-    for side in range(2):
-        for half in range(2):
-            for k in range(WINDOW):
-                for y in range(YS):
-                    if not is_own(half, k, y):
-                        table_copy(side, half, k, y).wait_send()
-
-    for slot in far_first:
-        every_copy(slot).wait_send()
-    for step in steps_far_first:
-        raw_copy(step).wait_send()
-        near_copy(step).wait_send()
-    for step in steps_far_first + (0,):
-        for half in range(2):
-            far_copy(half, step).wait_send()
 
 
 def per_device(shear, weight, partner_tiles, pair_count, pair_bin, pair_angle):

time: 38.3 us -> 38.1 us (level)
  no operation moved by 1% of the time
where the time goes in v7:
time: 38.1 us; the launch traced here: 38 us
  Pallas kernels  36.7 us (96%)
  local copies, waits for them, and re-layouts  0.72 us (2%)
  between operations  0.66 us (2%)
    pallas_call x1, Pallas kernels, per_device(): pl.pallas_call(kernel, out_shape=vmem((2 * LEGS * LEGS // LANES, LANES),...  36.7 us

profile of v7, /device:TPU:1, one launch (start us, length us, event | category | flops | bytes accessed | tf_op | source)
XLA Modules:
  0.0 38.0 jit_solution(610566717316402419)
XLA Ops:
  0.7 36.7 %shear_triples.1 = f32[576,128]{1,0:T(8,128)S(1)} custom-call(f32[1,2,32]{2,1,0:T(2,128)} %shear_in.1, f32[1,32]{1,0:T(1,128)} %weight_in.1, s32[1,4]{1,0:T(1,128)} %partners_in.1, s32[1,1]{1,0:T(1,128)} %bitcast.2.count_in, s32[1,256,128]{2,1,0:T(8,128)} %bins_in.1, f32[1,256,128]{2,1,0:T(8,128)} %angles_in.1), custom_call_target="tpu_custom_call" | custom-call | flops 800000000 | bytes 2000000 | tf_op jit(solution)/shard_map/shear_triples/pallas_call | solution.py:395
  37.3 0.7 %copy.8 = f32[1,1,73728]{2,1,0:T(1,128)} copy(f32[1,1,73728]{2,1,0:T(1,128)S(1)} %bitcast.3) | data formatting | bytes 589824
